TPU v7x, 32 devices: a whole 2x2x4 slice. The times are simulated.
32 devices in a mesh: dp: 16 (over z, x, core), group: 2 (over y).
Axes of the slice: x: 2, y: 2, z: 4, core: 2. Of those that a mesh axis runs over, the one named last changes fastest.
Arguments:
- tokens: bfloat16 [16384, 768], P(('dp', 'group')), may hold values from -6 to 6
- lengths: int32 [16], P('dp'), may hold values from 512 to 1024, as said below
- cotangent: bfloat16 [16384, 768], P(('dp', 'group')), may hold values from -6 to 6
- w_query: bfloat16 [768, 768], replicated, may hold values from -0.109375 to 0.109375
- w_keys: bfloat16 [768, 768], replicated, may hold values from -0.109375 to 0.109375
- w_values: bfloat16 [768, 768], replicated, may hold values from -0.21875 to 0.21875
- w_output: bfloat16 [768, 768], replicated, may hold values from -1.25 to 1.25
- w_gate: bfloat16 [768, 2048], replicated, may hold values from -0.21875 to 0.21875
- w_up: bfloat16 [768, 2048], replicated, may hold values from -0.21875 to 0.21875
- w_down: bfloat16 [2048, 768], replicated, may hold values from -0.1875 to 0.1875
- gain_attn: bfloat16 [768], replicated, may hold values from 0.5 to 1.5
- gain_ffn: bfloat16 [768], replicated, may hold values from 0.5 to 1.5
- bias_table: bfloat16 [32, 12], replicated, may hold values from -3 to 3
- master: float32 [55328, 128], P(('dp', 'group')), may hold values from -0.15625 to 0.15625
- moment_one: float32 [55328, 128], P(('dp', 'group')), may hold values from -64 to 64
- moment_two: float32 [55328, 128], P(('dp', 'group')), may hold values from 1 to 10000
Outputs:
- layer_out: bfloat16 [16384, 768], P(('dp', 'group'))
- grad_tokens: float32 [16384, 768], P(('dp', 'group'))
- grad_flat: float32 [55328, 128], P(('dp', 'group'))
- moment_one_new: float32 [55328, 128], P(('dp', 'group'))
- moment_two_new: float32 [55328, 128], P(('dp', 'group'))
- master_new: float32 [55328, 128], P(('dp', 'group'))
- fresh_copy: bfloat16 [55328, 128], replicated
Inputs may be any that keep to these rules, and one draw needn't show every extreme that they name: `lengths`: each slot's live tokens are a prefix of it; some slot is full.
All inputs are finite; a program needn't handle non-finite values.
Results may differ from a plain program's by a relative error of at most 0.015.
The roundings to bfloat16 on the way count: a program that leaves them out, or rounds other values in their place, can miss the bound.
Values may be sent and summed in bfloat16 or wider, within the bound.
A program may use at most 320 MiB of HBM per device.

v0:
```python
import jax
import jax.numpy as jnp
import numpy as np
from jax import lax
from jax.sharding import PartitionSpec as P

far_steps = np.array([8, 12, 16, 23, 32, 46, 64, 91], dtype=np.int32)
root_half = 0.7978845608028654


def bucket_index(offset):
    distance = jnp.abs(offset)
    passed = jnp.sum((distance[:, None] >= far_steps[None, :]).astype(jnp.int32), axis=1)
    inside = jnp.where(distance < 8, distance, 7 + passed)
    return inside + 16 * (offset > 0).astype(jnp.int32)


def rms_scale(values_in, gain_in):
    return (
        values_in
        * lax.rsqrt(jnp.mean(values_in * values_in, axis=-1, keepdims=True) + 1e-06)
        * gain_in
    )


def gelu_tanh(values_in):
    return (
        0.5
        * values_in
        * (1.0 + jnp.tanh(root_half * (values_in + 0.044715 * values_in * values_in * values_in)))
    )


def gated_product(gate_in, up_in):
    return gelu_tanh(gate_in) * up_in


def matmul(left_op, right_op):
    return jnp.dot(left_op, right_op, preferred_element_type=jnp.float32)


def product_tn(left_op, right_op):
    return lax.dot_general(
        left_op, right_op, (((0,), (0,)), ((), ())), preferred_element_type=jnp.float32
    )


def product_nt(left_op, right_op):
    return lax.dot_general(
        left_op, right_op, (((1,), (1,)), ((), ())), preferred_element_type=jnp.float32
    )


def skew_bias(table_wide, start_pos, block_rows, slot_span):
    width_all = block_rows + slot_span
    offsets = jnp.arange(width_all, dtype=jnp.int32) - (block_rows - 1) - start_pos
    buckets = bucket_index(offsets)
    onehot = (buckets[:, None] == jnp.arange(table_wide.shape[0], dtype=jnp.int32)[None, :]).astype(
        jnp.float32
    )
    per_offset = jnp.sum(onehot[:, :, None] * table_wide[None, :, :], axis=1)
    repeated = jnp.tile(per_offset.T, (1, block_rows))
    window = lax.slice_in_dim(
        repeated, block_rows - 1, block_rows - 1 + block_rows * (width_all - 1), axis=1
    )
    return (
        window.reshape(table_wide.shape[1], block_rows, width_all - 1)[:, :, :slot_span],
        onehot,
    )


def skew_grad(grad_scores, onehot, block_rows, slot_span):
    head_count = grad_scores.shape[0]
    width_all = block_rows + slot_span
    padded = jnp.pad(grad_scores, ((0, 0), (0, 0), (0, block_rows - 1)))
    flat_rows = padded.reshape(head_count, block_rows * (width_all - 1))
    flat_rows = jnp.pad(flat_rows, ((0, 0), (block_rows - 1, 1)))
    per_offset = jnp.sum(
        flat_rows.reshape(head_count, block_rows, width_all), axis=1, dtype=jnp.float32
    )
    return jnp.sum(onehot[:, :, None] * per_offset.T[:, None, :], axis=0)


def block_scores(query_block, key_heads, rel_bias, key_live):
    scores = (
        jnp.einsum("qhd,khd->hqk", query_block, key_heads, preferred_element_type=jnp.float32)
        + rel_bias
    )
    return jnp.where(key_live[None, None, :], scores, -jnp.inf)


def per_device(
    tokens,
    lengths,
    cotangent,
    w_query,
    w_keys,
    w_values,
    w_output,
    w_gate,
    w_up,
    w_down,
    gain_attn,
    gain_ffn,
    bias_table,
    master,
    moment_one,
    moment_two,
):
    local_rows, width = tokens.shape
    head_count = bias_table.shape[1]
    head_size = width // head_count
    group_size = lax.axis_size("group")
    slot_span = local_rows * group_size
    live_length = lengths[0]
    first_row = lax.axis_index("group") * local_rows
    block_rows = min(512, local_rows)
    key_live = jnp.arange(slot_span, dtype=jnp.int32) < live_length
    row_live = first_row + jnp.arange(local_rows, dtype=jnp.int32) < live_length
    table_wide = bias_table.astype(jnp.float32)
    inputs_wide = tokens.astype(jnp.float32)
    normed, attn_norm_pull = jax.vjp(rms_scale, inputs_wide, gain_attn.astype(jnp.float32))
    normed_low = normed.astype(jnp.bfloat16)
    query_rows = matmul(normed_low, w_query).astype(jnp.bfloat16)
    key_rows = matmul(normed_low, w_keys).astype(jnp.bfloat16)
    value_rows = matmul(normed_low, w_values).astype(jnp.bfloat16)
    all_keys, all_values = (
        lax.all_gather(key_rows, "group", axis=0, tiled=True),
        lax.all_gather(value_rows, "group", axis=0, tiled=True),
    )
    key_heads = all_keys.reshape(slot_span, head_count, head_size)
    value_heads = all_values.reshape(slot_span, head_count, head_size)
    query_heads = query_rows.reshape(local_rows, head_count, head_size)
    block_id = 0
    row_start = block_id * block_rows
    rel_bias, onehot = skew_bias(table_wide, first_row + row_start, block_rows, slot_span)
    scores = block_scores(query_heads, key_heads, rel_bias, key_live)
    row_max = jnp.max(scores, axis=2, keepdims=True)
    row_total = jnp.sum(jnp.exp(scores - row_max), axis=2, keepdims=True)
    log_total = row_max + jnp.log(row_total)
    prob_low = jnp.exp(scores - log_total).astype(jnp.bfloat16)
    mixed_blocks = jnp.einsum(
        "hqk,khd->qhd", prob_low, value_heads, preferred_element_type=jnp.float32
    )
    log_totals = [log_total]
    mixed_low = mixed_blocks.reshape(local_rows, width).astype(jnp.bfloat16)
    hidden_state = inputs_wide + matmul(mixed_low, w_output)
    normed_ffn, ffn_norm_pull = jax.vjp(rms_scale, hidden_state, gain_ffn.astype(jnp.float32))
    normed_ffn_low = normed_ffn.astype(jnp.bfloat16)
    gate_act = matmul(normed_ffn_low, w_gate)
    up_act = matmul(normed_ffn_low, w_up)
    inner_act, gated_pull = jax.vjp(gated_product, gate_act, up_act)
    inner_low = inner_act.astype(jnp.bfloat16)
    layer_out = (hidden_state + matmul(inner_low, w_down)).astype(jnp.bfloat16)
    grad_out = jnp.where(row_live[:, None], cotangent, jnp.zeros_like(cotangent))
    grad_w_down = product_tn(inner_low, grad_out)
    grad_inner = product_nt(grad_out, w_down)
    grad_gate, grad_up = gated_pull(grad_inner)
    grad_gate_low = grad_gate.astype(jnp.bfloat16)
    grad_up_low = grad_up.astype(jnp.bfloat16)
    grad_w_gate = product_tn(normed_ffn_low, grad_gate_low)
    grad_w_up = product_tn(normed_ffn_low, grad_up_low)
    grad_normed_ffn = product_nt(grad_gate_low, w_gate) + product_nt(grad_up_low, w_up)
    grad_from_norm, grad_gain_ffn = ffn_norm_pull(grad_normed_ffn)
    grad_hidden = grad_out.astype(jnp.float32) + grad_from_norm
    grad_branch = grad_hidden.astype(jnp.bfloat16)
    grad_w_output = product_tn(mixed_low, grad_branch)
    grad_mixed = product_nt(grad_branch, w_output).astype(jnp.bfloat16)
    grad_mixed_heads = grad_mixed.reshape(local_rows, head_count, head_size)
    block_id = 0
    row_start = block_id * block_rows
    rel_bias, onehot = skew_bias(table_wide, first_row + row_start, block_rows, slot_span)
    scores = block_scores(query_heads, key_heads, rel_bias, key_live)
    prob_full = jnp.exp(scores - log_totals[block_id])
    prob_low = prob_full.astype(jnp.bfloat16)
    grad_probs = jnp.einsum(
        "qhd,khd->hqk", grad_mixed_heads, value_heads, preferred_element_type=jnp.float32
    )
    row_inner = jnp.sum(prob_full * grad_probs, axis=2, keepdims=True)
    grad_scores = (prob_full * (grad_probs - row_inner)).astype(jnp.bfloat16)
    grad_query_blocks = jnp.einsum(
        "hqk,khd->qhd", grad_scores, key_heads, preferred_element_type=jnp.float32
    )
    grad_keys_part = jnp.einsum(
        "hqk,qhd->khd", grad_scores, query_heads, preferred_element_type=jnp.float32
    )
    grad_values_part = jnp.einsum(
        "hqk,qhd->khd", prob_low, grad_mixed_heads, preferred_element_type=jnp.float32
    )
    grad_table = skew_grad(grad_scores, onehot, block_rows, slot_span)
    grad_keys_own, grad_values_own = (
        lax.psum_scatter(
            grad_keys_part.astype(jnp.bfloat16), "group", scatter_dimension=0, tiled=True
        ).astype(jnp.float32),
        lax.psum_scatter(
            grad_values_part.astype(jnp.bfloat16), "group", scatter_dimension=0, tiled=True
        ).astype(jnp.float32),
    )
    grad_query_low = grad_query_blocks.reshape(local_rows, width).astype(jnp.bfloat16)
    grad_keys_low = grad_keys_own.reshape(local_rows, width).astype(jnp.bfloat16)
    grad_values_low = grad_values_own.reshape(local_rows, width).astype(jnp.bfloat16)
    grad_w_query = product_tn(normed_low, grad_query_low)
    grad_w_keys = product_tn(normed_low, grad_keys_low)
    grad_w_values = product_tn(normed_low, grad_values_low)
    grad_normed = (
        product_nt(grad_query_low, w_query)
        + product_nt(grad_keys_low, w_keys)
        + product_nt(grad_values_low, w_values)
    )
    grad_from_attn, grad_gain_attn = attn_norm_pull(grad_normed)
    grad_tokens = grad_hidden + grad_from_attn
    members = [
        grad_w_query,
        grad_w_keys,
        grad_w_values,
        grad_w_output,
        grad_w_gate,
        grad_w_up,
        grad_w_down,
        grad_gain_attn,
        grad_gain_ffn,
        grad_table,
    ]
    flat_grads = jnp.concatenate([member.reshape(-1) for member in members])
    shard_rows = master.shape[0]
    data_count = lax.axis_size("dp")
    total_rows = shard_rows * data_count * group_size
    flat_grads = jnp.pad(flat_grads, (0, total_rows * 128 - flat_grads.shape[0])).reshape(
        total_rows, 128
    )
    grad_shard = lax.psum_scatter(flat_grads, ("dp", "group"), scatter_dimension=0, tiled=True)
    moment_one_new = 0.9 * moment_one + 0.1 * grad_shard
    moment_two_new = 0.999 * moment_two + 0.001 * grad_shard * grad_shard
    first_hat = moment_one_new / (1.0 - 0.9**10)
    second_hat = moment_two_new / (1.0 - 0.999**10)
    master_new = master - 0.01 * (first_hat / (jnp.sqrt(second_hat) + 1e-08) + 0.1 * master)
    fresh_low = master_new.astype(jnp.bfloat16)
    fresh_copy = lax.all_gather(fresh_low, ("dp", "group"), axis=0, tiled=True)
    return (
        layer_out,
        grad_tokens,
        grad_shard,
        moment_one_new,
        moment_two_new,
        master_new,
        fresh_copy,
    )


def solution(mesh):
    return jax.shard_map(
        per_device,
        mesh=mesh,
        in_specs=(
            P(("dp", "group"), None),
            P("dp"),
            P(("dp", "group"), None),
            P(),
            P(),
            P(),
            P(),
            P(),
            P(),
            P(),
            P(),
            P(),
            P(),
            P(("dp", "group"), None),
            P(("dp", "group"), None),
            P(("dp", "group"), None),
        ),
        out_specs=(
            P(("dp", "group"), None),
            P(("dp", "group"), None),
            P(("dp", "group"), None),
            P(("dp", "group"), None),
            P(("dp", "group"), None),
            P(("dp", "group"), None),
            P(),
        ),
        check_vma=False,
    )
```

profile of v0, /device:TPU:0, one launch (start us, length us, event | category | flops | bytes accessed | tf_op | source)
XLA Modules:
  0.0 1389.0 jit_solution(2006216571801231871)
XLA Ops:
  10.1 3.2 convolution_convert_fusion.2
  13.4 3.2 convolution_convert_fusion.4
  18.0 12.9 tile.8
  30.9 30.3 %pad.16 = f32[16,512,1536]{2,1,0:T(8,128)} pad(f32[12,512,1536]{2,1,0:T(8,128)} %tile.8, f32[]{:T(128)} %constant.26.clone.1), padding=0_4x0_0x0_0 | pad | bytes 88080384
  61.2 46.1 %copy.50 = f32[2,8,512,1536]{3,1,2,0:T(8,128)} copy(f32[2,8,512,1536]{3,2,1,0:T(8,128)} %bitcast.80) | data formatting | bytes 100663296
  107.3 37.7 %slice.16 = f32[12,785920]{1,0:T(8,128)} slice(f32[12,786432]{1,0:T(8,128)} %bitcast.81), slice={[0:12], [511:786431]} | slice | bytes 75448320 | tf_op jit(solution)/shard_map/slice | solution.py:63
  145.0 66.9 %reshape.210 = f32[12,512,1535]{2,1,0:T(8,128)} reshape(f32[12,785920]{1,0:T(8,128)} %slice.16) | data formatting | bytes 75448320 | tf_op jit(solution)/shard_map/reshape | solution.py:67
  211.8 3.2 convolution_convert_fusion.3
  220.7 17.1 %fusion.53 = (f32[12,512]{1,0:T(8,128)S(1)}, f32[12,512,1024]{2,1,0:T(8,128)}) fusion(f32[12,512,1535]{2,1,0:T(8,128)} %reshape.210, bf16[512,12,64]{0,2,1:T(8,128)(2,1)} %bitcast.95, bf16[1024,12,64]{0,2,1:T(8,128)(2,1)} %bitcast.91, pred[1024]{0:T(1024)(128)(4,1)S(1)} %iota_compare_fusion.1), kind=kOutput, calls=%fused_computation.103 | convolution fusion | flops 824174592 | bytes 52716544 | tf_op jit(solution)/shard_map/qhd,khd->hqk/dot_general | solution.py:86
  237.8 10.9 exponential_reduce_fusion
  251.3 10.9 fusion.28
  269.0 8.4 multiply_convert_fusion.1
  287.8 16.5 %multiply_reduce_fusion = (f32[12,512]{1,0:T(8,128)S(1)}, f32[12,512,1024]{2,1,0:T(8,128)}) fusion(f32[12,512,1024]{2,1,0:T(8,128)} %get-tuple-element.20, f32[12,512]{1,0:T(8,128)S(1)} %log_add_fusion, bf16[512,12,64]{0,2,1:T(8,128)(2,1)} %bitcast.97, bf16[1024,12,64]{0,2,1:T(8,128)(2,1)} %bitcast.94), kind=kOutput, calls=%fused_computation.6 | convolution fusion | flops 824174592 | bytes 52740096 | tf_op jit(solution)/shard_map/qhd,khd->hqk/dot_general | solution.py:176
  304.2 21.5 %multiply_convert_fusion = bf16[12,512,1024]{2,1,0:T(8,128)(2,1)} fusion(f32[12,512,1024]{2,1,0:T(8,128)} %get-tuple-element.25, f32[12,512,1024]{2,1,0:T(8,128)} %get-tuple-element.20, f32[12,512]{1,0:T(8,128)S(1)} %get-tuple-element.24, f32[12,512]{1,0:T(8,128)S(1)} %log_add_fusion), kind=kLoop, calls=%fused_computation.5 | loop fusion | flops 25165824 | bytes 62963712 | tf_op jit(solution)/shard_map/convert_element_type | solution.py:180
  325.8 9.5 convolution_convert_fusion.5
  335.2 8.1 fusion.24
  343.4 3.9 fusion.47
  350.5 11.6 pad.12
  362.0 69.3 %reshape.220 = bf16[12,785920]{1,0:T(8,128)(2,1)} reshape(bf16[12,512,1535]{2,1,0:T(8,128)(2,1)} %pad.12) | data formatting | bytes 37724160 | tf_op jit(solution)/shard_map/reshape | solution.py:76
  431.4 27.7 %pad_convert_fusion = f32[12,786432]{1,0:T(8,128)} fusion(bf16[12,785920]{1,0:T(8,128)(2,1)} %reshape.220), kind=kLoop, calls=%fused_computation.4 | loop fusion | flops 9437184 | bytes 56610816 | tf_op jit(solution)/shard_map/convert_element_type | solution.py:78
  461.8 4.5 convolution_bitcast_fusion.1
  466.4 4.5 convolution_bitcast_fusion
  470.8 11.6 fusion.25
  482.5 3.9 fusion.32
  486.3 3.2 reshape.216
  489.5 7.4 copy.51
  496.9 7.2 copy.52
  504.1 4.6 fusion.41
  508.7 6.9 reshape.219
  515.6 45.9 %copy.53 = f32[2,8,512,1536]{3,2,1,0:T(8,128)} copy(f32[2,8,512,1536]{3,1,2,0:T(8,128)} %bitcast.79) | data formatting | bytes 100663296
  561.5 13.4 slice_reduce_fusion
  575.3 3.5 fusion.57
  578.8 3.8 fusion.45
  582.6 3.4 reshape.214
  586.0 3.5 fusion.58
  589.6 3.8 fusion.43
  593.3 3.2 reshape.215
  596.6 5.1 fusion.19
  607.9 3.4 constant_dynamic-update-slice_fusion.5
  622.5 21.7 %pad_bitcast_fusion = f32[55328,128]{1,0:T(8,128)} fusion(f32[7079808]{0:T(1024)} %constant_dynamic-update-slice_fusion), kind=kLoop, calls=%fused_computation.1 | loop fusion | bytes 56647168 | tf_op jit(solution)/shard_map/reshape | solution.py:228
  644.2 598.1 %fusion = f32[1744,128]{1,0:T(8,128)} fusion(f32[55328,128]{1,0:T(8,128)} %pad_bitcast_fusion), kind=kCustom, calls=%all-reduce-scatter | all-reduce-scatter fusion | flops 7143425 | bytes 29220864
  1244.0 7.0 collective-permute-start
  1251.0 5.1 collective-permute-done
  1256.0 4.1 concatenate.4
  1260.1 4.2 convert_bitcast_fusion
  1264.4 4.9 add_convert_fusion
  1270.8 99.9 %all-gather.9.cloned.1.call-done = bf16[32,1729,128]{2,1,0:T(8,128)(2,1)} async-done(((bf16[1,1729,128]{2,1,0:T(8,128)(2,1)}), bf16[32,1729,128]{2,1,0:T(8,128)(2,1)}) %all-gather.9.cloned.1.call-update) | async-done | bytes 14163984 | tf_op jit(solution)/shard_map/all_gather | solution.py:238
  1370.7 11.6 reshape.225
  (144 shorter events, 55.9 us)
Async XLA Ops:
  7.2 261.8 %copy-start = (bf16[2048,768]{1,0:T(8,128)(2,1)S(1)}, bf16[2048,768]{1,0:T(8,128)(2,1)}, u32[]{:S(2)}) copy-start(bf16[2048,768]{1,0:T(8,128)(2,1)} %param.27) | copy-start | bytes 9437188
  7.2 210.9 %all-gather.7.cloned.1.call-start = ((), (), s32[]{:S(2)}) async-start(), calls=%async_computation.3 | async-start | bytes 2359296 | tf_op jit(solution)/shard_map/all_gather | solution.py:128
  9.5 0.6 copy-start.26
  13.3 3.4 copy-start.28
  13.3 3.4 copy-start.31
  13.4 235.3 %all-gather.5.cloned.1.call-start = ((), (), s32[]{:S(2)}) async-start(), calls=%async_computation.2 | async-start | bytes 2359296 | tf_op jit(solution)/shard_map/all_gather | solution.py:129
  16.7 562.2 %reduce-scatter.5.cloned.1.call-start = ((), (), s32[]{:S(2)}) async-start(), calls=%async_computation.4 | async-start | bytes 2359296 | tf_op jit(solution)/shard_map/reduce_scatter | solution.py:192
  16.9 0.7 copy-start.24
  211.8 6.2 copy-start.30
  251.3 10.9 copy-start.1
  251.3 10.9 copy-start.34
  262.2 1.0 copy-start.18
  262.2 2.7 copy-start.32
  263.2 18.8 %copy-start.14 = (f32[512,768]{1,0:T(8,128)}, f32[512,768]{1,0:T(8,128)S(1)}, u32[]{:S(2)}) copy-start(f32[512,768]{1,0:T(8,128)S(1)} %get-tuple-element.22) | copy-start | bytes 4718596
  265.0 1.8 copy-start.11
  265.0 2.2 copy-start.33
  267.1 1.8 copy-start.16
  277.4 1.9 copy-start.22
  277.4 1.9 copy-start.20
  282.0 1.8 copy-start.35
  282.5 1.2 copy-start.4
  304.2 21.5 %copy-start.3 = (bf16[1024,768]{0,1:T(8,128)(2,1)S(1)}, bf16[1024,768]{0,1:T(8,128)(2,1)}, u32[]{:S(2)}) copy-start(bf16[1024,768]{0,1:T(8,128)(2,1)} %copy.47) | copy-start | bytes 4718596
  325.8 9.5 copy-start.10
  343.3 246.2 %reduce-scatter.7.cloned.1.call-start = ((), (), s32[]{:S(2)}) async-start(), calls=%async_computation.5 | async-start | bytes 2359296 | tf_op jit(solution)/shard_map/reduce_scatter | solution.py:195
  431.4 27.7 %copy-start.9 = (f32[589824]{0:T(1024)S(1)}, f32[589824]{0:T(1024)}, u32[]{:S(2)}) copy-start(f32[589824]{0:T(1024)} %reshape.213) | copy-start | bytes 7077892
  459.1 1.5 copy-start.12
  459.1 2.7 copy-start.23
  461.8 4.5 copy-start.21
  466.4 4.5 copy-start.13
  482.4 888.3 %all-gather.9.cloned.1.call-start = ((), (), s32[]{:S(2)}) async-start(), calls=%async_computation.6 | async-start | bytes 14665728 | tf_op jit(solution)/shard_map/all_gather | solution.py:238
  496.9 7.2 copy-start.17
  496.9 7.2 copy-start.19
  561.5 13.4 copy-start.25
  596.6 5.1 copy-start.7
  596.6 6.7 copy-start.8
  601.7 6.2 slice-start.2
  603.3 3.0 copy-start.6
  603.3 4.6 slice-start.3
  606.3 5.0 slice-start
  607.9 4.3 slice-start.1
  607.9 7.4 slice-start.4
  611.3 4.4 slice-start.5
  615.8 4.1 copy-start.29
  1244.0 12.0 collective-permute-start
  1264.3 4.9 copy-start.27
  1264.3 4.9 copy-start.2
  1264.3 4.9 copy-start.5
  1264.3 4.9 copy-start.15
Sparse Core Ops, SparseCore 0:
  13.5 29.8 all-gather.6
  45.5 27.2 all-gather.4
  343.4 28.6 reduce-scatter.4
  482.5 29.1 reduce-scatter.6
  1264.4 106.2 all-gather.8
where the time goes:
time: 1400 us; the launch traced here: 1390 us
  blocking collectives  598 us (43%)
  local copies, waits for them, and re-layouts  432 us (31%)
  matrix products  148 us (11%)
  waiting for transfers between devices  105 us (8%)
  other arithmetic  83.2 us (6%)
  between operations  15.2 us (1%)
    unnamed x1, blocking collectives  598 us
    unnamed x101, local copies, waits for them, and re-layouts  181 us
    all_gather x1, waiting for transfers between devices, per_device(): fresh_copy = lax.all_gather(fresh_low, ('dp', 'group'), axis=0, tiled=True)  99.9 us
    reshape x1, local copies, waits for them, and re-layouts, skew_grad(): flat_rows = padded.reshape(head_count, block_rows * (width_all - 1))  69.3 us
    reshape x1, local copies, waits for them, and re-layouts, skew_bias(): window.reshape(table_wide.shape[1], block_rows, width_all - 1)  66.9 us
    slice x1, local copies, waits for them, and re-layouts, skew_bias(): lax.slice_in_dim(repeated, block_rows - 1, block_rows - 1 + block_rows *...  37.7 us
    dot_general x7, matrix products, product_tn(): lax.dot_general(left_op, right_op, (((0,), (0,)), ((), ())), preferred_el...  28.8 us
  transfers between devices with their start and end apart: 6, of which 2 were waited for; matrix products, arithmetic and copies ran while one was open for 35% of the time, Pallas kernels for 0%

commit v1 on v0

--- a/solution.py
+++ b/solution.py
@@ -1,8 +1,336 @@
+import functools
 import jax
 import jax.numpy as jnp
 import numpy as np
 from jax import lax
+from jax.experimental import pallas as pl
+from jax.experimental.pallas import tpu as pltpu
 from jax.sharding import PartitionSpec as P
+
+MESH = pl.DeviceIdType.MESH
+bf16, f32 = jnp.bfloat16, jnp.float32
+
+
+class Grid:
+    def __init__(self, dp):
+        half = dp // 2
+        self.X = 1
+        while self.X * self.X * 4 <= half:
+            self.X *= 2
+        self.planes = half // self.X
+        self.devices = dp * 2
+        self.swap = self.X == 2
+
+    def here(self):
+        dp = lax.axis_index("dp")
+        self.core = lax.rem(dp, 2)
+        self.x = lax.rem(dp // 2, self.X)
+        self.plane = dp // (2 * self.X)
+        self.y = lax.axis_index("group")
+        self.flip = self.core if self.swap else 0
+        if self.swap:
+            self.a = jnp.where(self.core == 0, self.x, self.y)
+            self.b = jnp.where(self.core == 0, self.y, self.x)
+        else:
+            self.a, self.b = self.x, self.y
+        return self
+
+    def xy(self, a, b):
+        if not self.swap:
+            return a, b
+        return jnp.where(self.core == 0, a, b), jnp.where(self.core == 0, b, a)
+
+    def device(self, plane=None, a=None, b=None, core=None):
+        plane = self.plane if plane is None else plane
+        a = self.a if a is None else a
+        b = self.b if b is None else b
+        x, y = self.xy(a, b)
+        core = self.core if core is None else core
+        return ((plane * self.X + x) * 2 + core, y)
+
+    def index(self, plane, x, core, y):
+        return ((plane * self.X + x) * 2 + core) * 2 + y
+
+    def partners(self):
+        found = [self.device(core=1 - self.core), self.device(b=1 - self.b)]
+        found += [self.device(a=lax.rem(self.a + d, self.X)) for d in range(1, self.X)]
+        found += [self.device(plane=lax.rem(self.plane + d, self.planes)) for d in range(1, self.planes)]
+        return found
+
+
+def enter(partners):
+    barrier = pltpu.get_barrier_semaphore()
+    for one in partners:
+        pl.semaphore_signal(barrier, inc=1, device_id=one, device_id_type=MESH)
+    pl.semaphore_wait(barrier, len(partners))
+
+
+def add_rows(out, terms, rows, block):
+    @pl.loop(0, rows // block)
+    def _(step):
+        part = pl.ds(pl.multiple_of(step * block, block), block)
+        total = terms[0][part, :].astype(f32)
+        for term in terms[1:]:
+            total = total + term[part, :].astype(f32)
+        out[part, :] = total.astype(out.dtype)
+
+
+def block_of(rows):
+    for tiles in range(12, 0, -1):
+        if rows % (16 * tiles) == 0:
+            return 16 * tiles
+
+
+class Scatter:
+    def __init__(self, grid, first, count, stride, window):
+        self.g, self.first, self.count, self.stride, self.window = grid, first, count, stride, window
+
+    def scratch(self):
+        g, n, w = self.g, self.count, self.window
+        dma = pltpu.SemaphoreType.DMA
+        return [
+            pltpu.VMEM((n, g.X, 2, w, 128), bf16),
+            pltpu.VMEM((n, g.X, 2, w, 128), bf16),
+            pltpu.VMEM((n, g.X - 1, 2, w, 128), bf16),
+            pltpu.VMEM((n, w, 128), bf16),
+            pltpu.VMEM((g.planes - 1, w, 128), bf16),
+            pltpu.VMEM((w, 128), bf16),
+            dma((n, g.X, 2)), dma((n, g.X, 2)), dma((n, g.X, 2)),
+            dma((n, g.X - 1, 2)), dma((n, g.X - 1, 2)),
+            dma((n,)), dma((n,)), dma((n,)), dma((g.planes - 1,)),
+        ]
+
+    def bind(self, flat, out, scratch):
+        (self.own, self.r1, self.r2, self.r3, self.r4, self.kept, self.lsem, self.s1, self.q1, self.s2,
+         self.q2, self.s3, self.q3, self.s4, self.q4) = scratch
+        self.flat, self.out = flat, out
+
+    def plane_of(self, k):
+        return self.first + lax.rem(self.g.plane + 1 + k, self.count)
+
+    def copies0(self, k):
+        g = self.g
+        q = self.plane_of(k)
+        for x in range(g.X):
+            for y in range(2):
+                there = pl.multiple_of(self.stride * g.index(q, x, 1 - g.core, y), 16)
+                here = pl.multiple_of(self.stride * g.index(q, x, g.core, y), 16)
+                yield (
+                    pltpu.make_async_remote_copy(
+                        self.flat.at[pl.ds(there, self.window), :], self.r1.at[k, x, y],
+                        self.s1.at[k, x, y], self.q1.at[k, x, y],
+                        device_id=g.device(core=1 - g.core), device_id_type=MESH),
+                    pltpu.make_async_copy(
+                        self.flat.at[pl.ds(here, self.window), :], self.own.at[k, x, y], self.lsem.at[k, x, y]),
+                    x, y)
+
+    def copies1(self, k):
+        g = self.g
+        for d in range(1, g.X):
+            a = lax.rem(g.a + d, g.X)
+            for b in range(2):
+                x, y = g.xy(a, b)
+                yield pltpu.make_async_remote_copy(
+                    self.own.at[k, x, y], self.r2.at[k, d - 1, b], self.s2.at[k, d - 1, b], self.q2.at[k, d - 1, b],
+                    device_id=g.device(a=a), device_id_type=MESH)
+
+    def copy2(self, k):
+        g = self.g
+        x, y = g.xy(g.a, 1 - g.b)
+        return pltpu.make_async_remote_copy(
+            self.own.at[k, x, y], self.r3.at[k], self.s3.at[k], self.q3.at[k],
+            device_id=g.device(b=1 - g.b), device_id_type=MESH)
+
+    def copy3(self, k):
+        g = self.g
+        q = self.plane_of(k)
+        slot = lax.rem(g.plane - q + g.planes, g.planes) - 1
+        slot = jnp.maximum(slot, 0)
+        return pltpu.make_async_remote_copy(
+            self.own.at[k, g.x, g.y], self.r4.at[slot], self.s4.at[k], self.q4.at[slot],
+            device_id=g.device(plane=q), device_id_type=MESH)
+
+    def step(self, stage, k):
+        g = self.g
+        block = block_of(self.window)
+        if stage == 0:
+            for far, near, x, y in self.copies0(k):
+                far.start()
+                near.start()
+        elif stage == 1:
+            for far, near, x, y in self.copies0(k):
+                near.wait()
+                far.wait()
+                add_rows(self.own.at[k, x, y], [self.own.at[k, x, y], self.r1.at[k, x, y]], self.window, block)
+            for copy in self.copies1(k):
+                copy.start()
+        elif stage == 2:
+            for copy in self.copies1(k):
+                copy.wait()
+            for b in range(2):
+                x, y = g.xy(g.a, b)
+                mine = self.own.at[k, x, y]
+                add_rows(mine, [mine] + [self.r2.at[k, d, b] for d in range(g.X - 1)], self.window, block)
+            self.copy2(k).start()
+        elif stage == 3:
+            self.copy2(k).wait()
+            mine = self.own.at[k, g.x, g.y]
+            q = self.plane_of(k)
+            add_rows(mine, [mine, self.r3.at[k]], self.window, block)
+
+            @pl.when(q != g.plane)
+            def _():
+                self.copy3(k).start()
+
+            @pl.when(q == g.plane)
+            def _():
+                add_rows(self.kept, [mine], self.window, block)
+
+    def finish(self):
+        g = self.g
+        for k in range(self.count):
+            @pl.when(self.plane_of(k) != g.plane)
+            def _():
+                self.copy3(k).wait_send()
+
+        inside = jnp.logical_and(g.plane >= self.first, g.plane < self.first + self.count)
+
+        @pl.when(inside)
+        def _():
+            for d in range(g.planes - 1):
+                pltpu.make_async_remote_copy(
+                    self.kept, self.r4.at[d], self.s4.at[0], self.q4.at[d],
+                    device_id=g.device(plane=lax.rem(g.plane + 1 + d, g.planes)), device_id_type=MESH).wait_recv()
+            add_rows(self.out, [self.kept] + [self.r4.at[d] for d in range(g.planes - 1)], self.window,
+                     block_of(self.window))
+
+        @pl.when(jnp.logical_not(inside))
+        def _():
+            self.out[...] = jnp.zeros_like(self.out)
+
+    def all(self):
+        for k in range(self.count):
+            self.step(0, k)
+        for t in range(self.count + 2):
+            for stage in (3, 2, 1):
+                k = t - (stage - 1)
+                if 0 <= k < self.count:
+                    self.step(stage, k)
+        self.finish()
+
+
+def scatter_kernel(grid, make, flat, out, *scratch):
+    grid.here()
+    enter(grid.partners())
+    job = make()
+    job.bind(flat, out, scratch)
+    job.all()
+
+
+def scatter_rows(flat, grid, first, count, stride, window, collective_id):
+    make = lambda: Scatter(grid, first, count, stride, window)
+    return pl.pallas_call(
+        functools.partial(scatter_kernel, grid, make),
+        out_shape=jax.ShapeDtypeStruct((window, 128), f32),
+        in_specs=[pl.BlockSpec(memory_space=pl.ANY)],
+        out_specs=pl.BlockSpec(memory_space=pltpu.VMEM),
+        scratch_shapes=make().scratch(),
+        compiler_params=pltpu.CompilerParams(
+            collective_id=collective_id, has_side_effects=True, vmem_limit_bytes=56 << 20),
+    )(flat)
+
+
+def gather_kernel(grid, stride, fresh, tail, out, lsem, tsem, s0, q0, s1, q1, s2, q2, s3, q3):
+    g = grid.here()
+    enter(g.partners())
+    X, planes = g.X, g.planes
+
+    def rows(q, x, core, y):
+        return out.at[pl.ds(pl.multiple_of(stride * g.index(q, x, core, y), 16), stride), :]
+
+    mine = rows(g.plane, g.x, g.core, g.y)
+    first = pltpu.make_async_copy(fresh, mine, lsem)
+    first.start()
+    rest = pltpu.make_async_copy(tail, out.at[pl.ds(stride * g.devices, g.devices), :], tsem)
+    rest.start()
+
+    def send0(d):
+        return pltpu.make_async_remote_copy(
+            fresh, mine, s0.at[d - 1], q0.at[d - 1],
+            device_id=g.device(plane=lax.rem(g.plane + d, planes)), device_id_type=MESH)
+
+    def plane_of(k):
+        return lax.rem(g.plane - k + planes, planes)
+
+    def send1(k):
+        part = rows(plane_of(k), g.x, g.core, g.y)
+        return pltpu.make_async_remote_copy(
+            part, part, s1.at[k], q1.at[k], device_id=g.device(b=1 - g.b), device_id_type=MESH)
+
+    def send2(k):
+        for d in range(1, X):
+            for b in range(2):
+                x, y = g.xy(g.a, b)
+                part = rows(plane_of(k), x, g.core, y)
+                yield pltpu.make_async_remote_copy(
+                    part, part, s2.at[k, d - 1, b], q2.at[k, d - 1, b],
+                    device_id=g.device(a=lax.rem(g.a + d, X)), device_id_type=MESH)
+
+    def send3(k):
+        for x in range(X):
+            for y in range(2):
+                part = rows(plane_of(k), x, g.core, y)
+                yield pltpu.make_async_remote_copy(
+                    part, part, s3.at[k, x, y], q3.at[k, x, y],
+                    device_id=g.device(core=1 - g.core), device_id_type=MESH)
+
+    for d in range(1, planes):
+        send0(d).start()
+    first.wait()
+    for t in range(planes + 2):
+        if t < planes:
+            if t > 0:
+                send0(t).wait_recv()
+            send1(t).start()
+        k = t - 1
+        if 0 <= k < planes:
+            send1(k).wait_recv()
+            for copy in send2(k):
+                copy.start()
+        k = t - 2
+        if 0 <= k < planes:
+            for copy in send2(k):
+                copy.wait_recv()
+            for copy in send3(k):
+                copy.start()
+    for k in range(planes):
+        for copy in send3(k):
+            copy.wait_recv()
+    for d in range(1, planes):
+        send0(d).wait_send()
+    for k in range(planes):
+        send1(k).wait_send()
+        for copy in send2(k):
+            copy.wait_send()
+        for copy in send3(k):
+            copy.wait_send()
+    rest.wait()
+
+
+def gather_rows(fresh, tail, grid, stride, collective_id):
+    dma = pltpu.SemaphoreType.DMA
+    n, X = grid.planes, grid.X
+    total = (stride + 1) * grid.devices
+    return pl.pallas_call(
+        functools.partial(gather_kernel, grid, stride),
+        out_shape=jax.ShapeDtypeStruct((total, 128), bf16),
+        in_specs=[pl.BlockSpec(memory_space=pl.ANY)] * 2,
+        out_specs=pl.BlockSpec(memory_space=pl.ANY),
+        scratch_shapes=[dma, dma, dma((n - 1,)), dma((n - 1,)), dma((n,)), dma((n,)),
+                        dma((n, X - 1, 2)), dma((n, X - 1, 2)), dma((n, X, 2)), dma((n, X, 2))],
+        compiler_params=pltpu.CompilerParams(collective_id=collective_id, has_side_effects=True),
+    )(fresh, tail)
+
 
 far_steps = np.array([8, 12, 16, 23, 32, 46, 64, 91], dtype=np.int32)
 root_half = 0.7978845608028654
@@ -87,6 +415,15 @@
         + rel_bias
     )
     return jnp.where(key_live[None, None, :], scores, -jnp.inf)
+
+
+def adam_step(grads, moment_one, moment_two, master):
+    moment_one_new = 0.9 * moment_one + 0.1 * grads
+    moment_two_new = 0.999 * moment_two + 0.001 * grads * grads
+    first_hat = moment_one_new / (1.0 - 0.9**10)
+    second_hat = moment_two_new / (1.0 - 0.999**10)
+    master_new = master - 0.01 * (first_hat / (jnp.sqrt(second_hat) + 1e-08) + 0.1 * master)
+    return moment_one_new, moment_two_new, master_new
 
 
 def per_device(
@@ -221,21 +558,38 @@
         grad_gain_ffn,
         grad_table,
     ]
-    flat_grads = jnp.concatenate([member.reshape(-1) for member in members])
     shard_rows = master.shape[0]
-    data_count = lax.axis_size("dp")
-    total_rows = shard_rows * data_count * group_size
-    flat_grads = jnp.pad(flat_grads, (0, total_rows * 128 - flat_grads.shape[0])).reshape(
-        total_rows, 128
-    )
-    grad_shard = lax.psum_scatter(flat_grads, ("dp", "group"), scatter_dimension=0, tiled=True)
-    moment_one_new = 0.9 * moment_one + 0.1 * grad_shard
-    moment_two_new = 0.999 * moment_two + 0.001 * grad_shard * grad_shard
-    first_hat = moment_one_new / (1.0 - 0.9**10)
-    second_hat = moment_two_new / (1.0 - 0.999**10)
-    master_new = master - 0.01 * (first_hat / (jnp.sqrt(second_hat) + 1e-08) + 0.1 * master)
-    fresh_low = master_new.astype(jnp.bfloat16)
-    fresh_copy = lax.all_gather(fresh_low, ("dp", "group"), axis=0, tiled=True)
+    grid = Grid(lax.axis_size("dp"))
+    count = grid.devices
+    stride, window = shard_rows - 1, shard_rows - 1 + count
+    place = lax.axis_index("dp") * group_size + lax.axis_index("group")
+    tail = jnp.concatenate([member.reshape(-1) for member in members[7:]])
+    tail = jnp.pad(tail, (0, count * 128 - tail.shape[0])).reshape(count, 128)
+    tail = lax.psum(tail, ("dp", "group"))
+    flat = jnp.concatenate([member.astype(bf16).reshape(-1, 128) for member in members[:7]])
+    flat = jnp.pad(flat, ((0, count), (0, 0)))
+    summed = scatter_rows(flat, grid, 0, grid.planes, stride, window, 1)
+    summed = jnp.where(
+        (place == count - 1) & (jnp.arange(window) >= stride)[:, None],
+        jnp.pad(tail, ((stride, 0), (0, 0))),
+        summed,
+    )
+    grad_shard = lax.dynamic_slice_in_dim(summed, place, shard_rows, 0)
+    moment_one_new, moment_two_new, master_new = adam_step(
+        grad_shard, moment_one, moment_two, master
+    )
+    states = (moment_one, moment_two, master)
+    ends = jnp.stack([state[shard_rows - count :] for state in states])
+    ring = [(one, (one + 1) % count) for one in range(count)]
+    before = lax.ppermute(ends, ("dp", "group"), ring)
+    last = lax.psum(jnp.where(place == count - 1, ends, 0.0), ("dp", "group"))
+    wide = [
+        lax.dynamic_slice_in_dim(jnp.concatenate([before[k], states[k]]), count - place, stride, 0)
+        for k in range(3)
+    ]
+    fresh = adam_step(summed[:stride], *wide)[2].astype(bf16)
+    fresh_tail = adam_step(tail, *last)[2].astype(bf16)
+    fresh_copy = gather_rows(fresh, fresh_tail, grid, stride, 2)
     return (
         layer_out,
         grad_tokens,

time: 1400 us -> 858 us (0.61)
  blocking collectives: 598 us -> 0 us
  Pallas kernels: 0 us -> 164 us
  waiting for transfers between devices: 105 us -> 23.1 us
  local copies, waits for them, and re-layouts: 432 us -> 414 us
    unnamed x1 -> x0, blocking collectives: 598 us -> none
    pallas_call x0 -> x2, Pallas kernels: none -> 164 us  [the longest x1 81.9 us: scatter_rows(): pl.pallas_call(functools.partial(scatter_kernel, grid, make), out_shape=j...]
    all_gather x1 -> x0, waiting for transfers between devices: 99.9 us -> none  [per_device(): fresh_copy = lax.all_gather(fresh_low, ('dp', 'group'), axis=0, tiled=True)]
    unnamed x101 -> x112, local copies, waits for them, and re-layouts: 181 us -> 157 us
    psum x0 -> x1, waiting for transfers between devices: none -> 23 us  [per_device(): tail = lax.psum(tail, ('dp', 'group'))]
    reshape x7 -> x8, local copies, waits for them, and re-layouts: 41.9 us -> 32 us  [the longest x7 31.9 us: per_device(): member.astype(bf16).reshape(-1, 128)]
  transfers between devices with their start and end apart: 6 -> 6, of which waited for: 2 -> 1; matrix products, arithmetic and copies ran while one was open for 35% -> 60% of each run, Pallas kernels for 0% -> 10%
where the time goes in v1:
time: 858 us; the launch traced here: 844 us
  local copies, waits for them, and re-layouts  414 us (48%)
  Pallas kernels  164 us (19%)
  matrix products  138 us (16%)
  other arithmetic  87 us (10%)
  waiting for transfers between devices  23.1 us (3%)
  between operations  15.2 us (2%)
    unnamed x112, local copies, waits for them, and re-layouts  157 us
    pallas_call x1, Pallas kernels, scatter_rows(): pl.pallas_call(functools.partial(scatter_kernel, grid, make), out_shape=j...  81.9 us
    pallas_call x1, Pallas kernels, gather_rows(): pl.pallas_call(functools.partial(gather_kernel, grid, stride), out_shape=...  81.8 us
    reshape x1, local copies, waits for them, and re-layouts, skew_grad(): flat_rows = padded.reshape(head_count, block_rows * (width_all - 1))  69.5 us
    reshape x1, local copies, waits for them, and re-layouts, skew_bias(): window.reshape(table_wide.shape[1], block_rows, width_all - 1)  66.5 us
    slice x1, local copies, waits for them, and re-layouts, skew_bias(): lax.slice_in_dim(repeated, block_rows - 1, block_rows - 1 + block_rows *...  37.7 us
    reshape x7, local copies, waits for them, and re-layouts, per_device(): member.astype(bf16).reshape(-1, 128)  31.9 us
    dot_general x7, matrix products, product_tn(): lax.dot_general(left_op, right_op, (((0,), (0,)), ((), ())), preferred_el...  28.5 us
  transfers between devices with their start and end apart: 6, of which 1 were waited for; matrix products, arithmetic and copies ran while one was open for 60% of the time, Pallas kernels for 10%

profile of v1, /device:TPU:0, one launch (start us, length us, event | category | flops | bytes accessed | tf_op | source)
XLA Modules:
  0.0 844.2 jit_solution(17866739147834812558)
XLA Ops:
  10.0 3.2 convolution_convert_fusion.9
  15.5 3.0 collective-permute-start
  18.4 3.2 convolution_convert_fusion.11
  22.5 3.5 convolution_convert_fusion.10
  27.6 12.7 %tile.8 = f32[12,512,1536]{2,1,0:T(8,128)} broadcast(f32[12,1536]{1,0:T(8,128)S(1)} %bitcast.123), dimensions={0,2} | broadcast | bytes 37822464 | tf_op jit(solution)/shard_map/tile | solution.py:390
  40.3 30.2 %pad.40 = f32[16,512,1536]{2,1,0:T(8,128)} pad(f32[12,512,1536]{2,1,0:T(8,128)} %tile.8, f32[]{:T(128)} %constant.33.clone.1), padding=0_4x0_0x0_0 | pad | bytes 88080384
  70.5 46.2 %copy.50 = f32[2,8,512,1536]{3,1,2,0:T(8,128)} copy(f32[2,8,512,1536]{3,2,1,0:T(8,128)} %bitcast.106) | data formatting | bytes 100663296
  116.6 37.7 %slice.44 = f32[12,785920]{1,0:T(8,128)} slice(f32[12,786432]{1,0:T(8,128)} %bitcast.107), slice={[0:12], [511:786431]} | slice | bytes 75448320 | tf_op jit(solution)/shard_map/slice | solution.py:391
  154.3 66.5 %reshape.220 = f32[12,512,1535]{2,1,0:T(8,128)} reshape(f32[12,785920]{1,0:T(8,128)} %slice.44) | data formatting | bytes 75448320 | tf_op jit(solution)/shard_map/reshape | solution.py:395
  226.3 17.1 %fusion.75 = (f32[12,512]{1,0:T(8,128)S(1)}, f32[12,512,1024]{2,1,0:T(8,128)}) fusion(f32[12,512,1535]{2,1,0:T(8,128)} %reshape.220, bf16[512,12,64]{0,2,1:T(8,128)(2,1)} %bitcast.113, bf16[1024,12,64]{0,2,1:T(8,128)(2,1)} %bitcast.109, pred[1024]{0:T(1024)(128)(4,1)S(1)} %iota_compare_fusion.3), kind=kOutput, calls=%fused_computation.151 | convolution fusion | flops 824174592 | bytes 52716544 | tf_op jit(solution)/shard_map/qhd,khd->hqk/dot_general | solution.py:414
  243.4 10.9 %exponential_reduce_fusion = f32[12,512]{1,0:T(8,128)S(1)} fusion(f32[12,512,1024]{2,1,0:T(8,128)} %get-tuple-element.26, f32[12,512]{1,0:T(8,128)S(1)} %get-tuple-element.25), kind=kLoop, calls=%fused_computation.7 | loop fusion | flops 12576768 | bytes 25214976 | tf_op jit(solution)/shard_map/reduce_sum | solution.py:476
  257.0 10.9 %fusion.27 = bf16[12,64,512]{2,1,0:T(8,128)(2,1)S(1)} fusion(bf16[1024,12,64]{0,2,1:T(8,128)(2,1)} %bitcast.111, f32[12,512,1024]{2,1,0:T(8,128)} %get-tuple-element.26, f32[12,512]{1,0:T(8,128)S(1)} %log_add_fusion), kind=kOutput, calls=%fused_computation.63 | convolution fusion | flops 818282496 | bytes 27549696 | tf_op jit(solution)/shard_map/hqk,khd->qhd/dot_general | solution.py:479
  274.6 8.2 multiply_convert_fusion.1
  284.9 2.7 multiply_reduce_fusion.3
  293.3 16.5 %multiply_reduce_fusion = (f32[12,512]{1,0:T(8,128)S(1)}, f32[12,512,1024]{2,1,0:T(8,128)}) fusion(f32[12,512,1024]{2,1,0:T(8,128)} %get-tuple-element.26, f32[12,512]{1,0:T(8,128)S(1)} %log_add_fusion, bf16[512,12,64]{0,2,1:T(8,128)(2,1)} %bitcast.115, bf16[1024,12,64]{0,2,1:T(8,128)(2,1)} %bitcast.112), kind=kOutput, calls=%fused_computation.5 | convolution fusion | flops 824174592 | bytes 52740096 | tf_op jit(solution)/shard_map/qhd,khd->hqk/dot_general | solution.py:513
  309.8 16.6 %multiply_convert_fusion = bf16[12,512,1024]{2,1,0:T(8,128)(2,1)S(1)} fusion(f32[12,512,1024]{2,1,0:T(8,128)} %get-tuple-element.31, f32[12,512,1024]{2,1,0:T(8,128)} %get-tuple-element.26, f32[12,512]{1,0:T(8,128)S(1)} %get-tuple-element.30, f32[12,512]{1,0:T(8,128)S(1)} %log_add_fusion), kind=kLoop, calls=%fused_computation.4 | loop fusion | flops 25165824 | bytes 62963712 | tf_op jit(solution)/shard_map/convert_element_type | solution.py:517
  326.4 4.8 copy-done.1
  331.2 3.5 fusion.23
  334.7 12.0 %pad.20 = bf16[12,512,1535]{2,1,0:T(8,128)(2,1)} pad(bf16[12,512,1024]{2,1,0:T(8,128)(2,1)} %copy-done.1, bf16[]{:T(256)} %constant.48.clone.1), padding=0_0x0_0x0_511 | pad | bytes 31444994 | tf_op jit(solution)/shard_map/jit(_pad)/pad | solution.py:403
  346.8 69.5 %reshape.223 = bf16[12,785920]{1,0:T(8,128)(2,1)} reshape(bf16[12,512,1535]{2,1,0:T(8,128)(2,1)} %pad.20) | data formatting | bytes 37724160 | tf_op jit(solution)/shard_map/reshape | solution.py:404
  416.3 27.7 %pad_convert_fusion = f32[12,786432]{1,0:T(8,128)} fusion(bf16[12,785920]{1,0:T(8,128)(2,1)} %reshape.223), kind=kLoop, calls=%fused_computation.3 | loop fusion | flops 9437184 | bytes 56610816 | tf_op jit(solution)/shard_map/convert_element_type | solution.py:406
  444.0 8.6 %convolution_convert_fusion.12 = bf16[12,64,512]{2,1,0:T(8,128)(2,1)S(1)} fusion(bf16[1024,12,64]{0,2,1:T(8,128)(2,1)S(1)} %bitcast.110, bf16[12,512,1024]{2,1,0:T(8,128)(2,1)} %copy-done.1), kind=kOutput, calls=%fused_computation.64 | convolution fusion | flops 805699584 | bytes 14942208 | tf_op jit(solution)/shard_map/hqk,khd->qhd/dot_general | solution.py:518
  455.4 3.3 reshape.226
  458.8 3.4 convolution_convert_fusion.4
  462.2 3.3 reshape.229
  465.6 5.3 convolution_convert_fusion.2
  470.9 5.9 reshape.230
  476.8 5.3 convolution_convert_fusion.1
  482.1 6.2 reshape.231
  488.4 5.3 convolution_convert_fusion
  493.7 6.4 reshape.232
  500.1 45.9 %copy.51 = f32[2,8,512,1536]{3,2,1,0:T(8,128)} copy(f32[2,8,512,1536]{3,1,2,0:T(8,128)} %bitcast.105) | data formatting | bytes 100663296
  546.0 11.8 %fusion.24 = bf16[1024,12,64]{0,2,1:T(8,128)(2,1)} fusion(bf16[512,12,64]{0,2,1:T(8,128)(2,1)} %bitcast.116, f32[12,512,1024]{2,1,0:T(8,128)} %get-tuple-element.26, f32[12,512]{1,0:T(8,128)S(1)} %log_add_fusion), kind=kOutput, calls=%fused_computation.57 | convolution fusion | flops 818675712 | bytes 27549696 | tf_op jit(solution)/shard_map/hqk,qhd->khd/dot_general | solution.py:524
  557.9 14.0 %slice_reduce_fusion = f32[12,1536]{1,0:T(8,128)S(1)} fusion(f32[16,512,1536]{2,1,0:T(8,128)} %bitcast.108), kind=kLoop, calls=%fused_computation | loop fusion | flops 9418752 | bytes 37822464 | tf_op jit(solution)/shard_map/reduce_sum | solution.py:406
  572.3 3.6 fusion.79
  576.0 2.7 add_convert_fusion
  579.8 3.5 convolution_convert_fusion.6
  585.3 3.5 convolution_convert_fusion.5
  588.9 4.0 fusion.18
  592.9 3.3 reshape.227
  596.2 3.3 reshape.228
  613.4 3.7 fusion.20
  617.1 12.8 %pad.24.flat = bf16[55328,128]{1,0:T(8,128)(2,1)} pad(bf16[55296,128]{1,0:T(8,128)(2,1)} %constant_dynamic-update-slice_fusion, bf16[]{:T(256)} %constant.48.clone.1), padding=0_32x0_0 | pad | bytes 28319746 | tf_op jit(solution)/shard_map/jit(_pad)/pad | solution.py:570
  629.9 81.9 %shard_map.225 = f32[1760,128]{1,0:T(8,128)} custom-call(bf16[55328,128]{1,0:T(8,128)(2,1)} %pad.24.flat), custom_call_target="tpu_custom_call" | custom-call | tf_op jit(solution)/shard_map/pallas_call | solution.py:232
  711.8 23.0 %all-reduce.8.cloned.1.call-done = (f32[32,128]{1,0:T(8,128)}, f32[3,32,128]{2,1,0:T(8,128)}) async-done(((f32[32,128]{1,0:T(8,128)}, f32[3,32,128]{2,1,0:T(8,128)}), (f32[32,128]{1,0:T(8,128)}, f32[3,32,128]{2,1,0:T(8,128)})) %all-reduce.8.cloned.1.call-update) | async-done | bytes 65552 | tf_op jit(solution)/shard_map/psum | solution.py:568
  737.8 3.2 multiply_subtract_fusion
  742.9 81.8 %shard_map.226 = bf16[55328,128]{1,0:T(8,128)(2,1)} custom-call(bf16[1728,128]{1,0:T(8,128)(2,1)} %subtract_convert_fusion.fresh, bf16[32,128]{1,0:T(8,128)(2,1)} %fusion.60.tail), custom_call_target="tpu_custom_call" | custom-call | tf_op jit(solution)/shard_map/pallas_call | solution.py:324
  824.7 12.8 %copy.62 = bf16[55328,128]{1,0:T(8,128)(2,1)} copy(bf16[55328,128]{1,0:T(8,128)(2,1)} %shard_map.226) | data formatting | bytes 28327936
  (164 shorter events, 54.5 us)
Async XLA Ops:
  7.2 267.5 %copy-start = (bf16[2048,768]{1,0:T(8,128)(2,1)S(1)}, bf16[2048,768]{1,0:T(8,128)(2,1)}, u32[]{:S(2)}) copy-start(bf16[2048,768]{1,0:T(8,128)(2,1)} %param.27) | copy-start | bytes 9437188
  7.2 216.5 %all-gather.5.cloned.1.call-start = ((), (), s32[]{:S(2)}) async-start(), calls=%async_computation.3 | async-start | bytes 2359296 | tf_op jit(solution)/shard_map/all_gather | solution.py:465
  8.1 14.4 %copy-start.30 = (f32[768]{0:T(1024)}, f32[768]{0:T(1024)S(1)}, u32[]{:S(2)}) copy-start(f32[768]{0:T(1024)S(1)} %convert_element_type.163) | copy-start | bytes 9220
  10.0 12.4 %copy-start.34 = (f32[512]{0:T(512)}, f32[512]{0:T(512)S(1)}, u32[]{:S(2)}) copy-start(f32[512]{0:T(512)S(1)} %fusion.65) | copy-start | bytes 6148
  13.3 241.1 %all-gather.3.cloned.1.call-start = ((), (), s32[]{:S(2)}) async-start(), calls=%async_computation.2 | async-start | bytes 2359296 | tf_op jit(solution)/shard_map/all_gather | solution.py:466
  15.5 6.8 copy-start.37
  15.5 6.8 copy-start.41
  15.5 207.6 %collective-permute-start = (f32[3,32,128]{2,1,0:T(8,128)S(1)}, f32[3,32,128]{2,1,0:T(8,128)S(1)}, u32[]{:S(2)}, u32[]{:S(2)}) collective-permute-start(f32[3,32,128]{2,1,0:T(8,128)S(1)} %get-tuple-element.23), channel_id=1, source_target_pairs={{0,1},{1,2},{2,3},{3,4},{4,5},{5,6},{6,7},{7,8},{8,9},{9,10},{10,1... | collective-permute-start | bytes 147464 | tf_op jit(solution)/shard_map/ppermute | solution.py:584
  21.7 558.1 %reduce-scatter.3.cloned.1.call-start = ((), (), s32[]{:S(2)}) async-start(), calls=%async_computation.4 | async-start | bytes 2359296 | tf_op jit(solution)/shard_map/reduce_scatter | solution.py:529
  22.5 4.6 copy-start.20
  154.3 68.8 %copy-start.39 = (bf16[768]{0:T(1024)(128)(2,1)S(1)}, bf16[768]{0:T(1024)(128)(2,1)}, u32[]{:S(2)}) copy-start(bf16[768]{0:T(1024)(128)(2,1)} %param.29) | copy-start | bytes 4612
  257.0 10.9 %copy-start.8 = (bf16[512,768]{1,0:T(8,128)(2,1)S(1)}, bf16[512,768]{1,0:T(8,128)(2,1)}, u32[]{:S(2)}) copy-start(bf16[512,768]{1,0:T(8,128)(2,1)} %param.18) | copy-start | bytes 2359300
  257.0 10.9 %copy-start.44 = (bf16[768,768]{1,0:T(8,128)(2,1)S(1)}, bf16[768,768]{1,0:T(8,128)(2,1)}, u32[]{:S(2)}) copy-start(bf16[768,768]{1,0:T(8,128)(2,1)} %param.24) | copy-start | bytes 3538948
  267.9 2.7 copy-start.42
  268.9 18.7 %copy-start.11 = (f32[512,768]{1,0:T(8,128)}, f32[512,768]{1,0:T(8,128)S(1)}, u32[]{:S(2)}) copy-start(f32[512,768]{1,0:T(8,128)S(1)} %get-tuple-element.28) | copy-start | bytes 4718596
  270.6 2.2 copy-start.43
  282.9 1.9 copy-start.49
  282.9 2.0 copy-start.48
  309.8 21.4 %copy-start.7 = (bf16[512,768]{0,1:T(8,128)(2,1)S(1)}, bf16[512,768]{0,1:T(8,128)(2,1)}, u32[]{:S(2)}) copy-start(bf16[512,768]{0,1:T(8,128)(2,1)} %copy.46) | copy-start | bytes 2359300
  326.4 4.8 copy-start.1
  334.7 250.6 %reduce-scatter.5.cloned.1.call-start = ((), (), s32[]{:S(2)}) async-start(), calls=%async_computation.5 | async-start | bytes 2359296 | tf_op jit(solution)/shard_map/reduce_scatter | solution.py:532
  416.3 27.7 %copy-start.2 = (bf16[1024,768]{0,1:T(8,128)(2,1)S(1)}, bf16[1024,768]{0,1:T(8,128)(2,1)}, u32[]{:S(2)}) copy-start(bf16[1024,768]{0,1:T(8,128)(2,1)} %copy.47) | copy-start | bytes 4718596
  444.0 9.5 %copy-start.9 = (bf16[512,768]{1,0:T(8,128)(2,1)S(1)}, bf16[512,768]{1,0:T(8,128)(2,1)}, u32[]{:S(2)}) copy-start(bf16[512,768]{1,0:T(8,128)(2,1)} %param.18) | copy-start | bytes 2359300
  444.0 9.5 %copy-start.31 = (f32[768]{0:T(1024)S(1)}, f32[768]{0:T(1024)}, u32[]{:S(2)}) copy-start(f32[768]{0:T(1024)} %copy-done.30) | copy-start | bytes 9220
  444.0 9.5 %copy-start.35 = (f32[512]{0:T(512)S(1)}, f32[512]{0:T(512)}, u32[]{:S(2)}) copy-start(f32[512]{0:T(512)} %copy-done.34) | copy-start | bytes 6148
  557.8 176.9 %all-reduce.8.cloned.1.call-start = ((), (), s32[]{:S(2)}) async-start(), calls=%async_computation.6 | async-start | bytes 131072 | tf_op jit(solution)/shard_map/psum | solution.py:568
  557.9 14.0 %copy-start.21 = (f32[1536,32]{0,1:T(8,128)S(1)}, f32[1536,32]{0,1:T(8,128)}, u32[]{:S(2)}) copy-start(f32[1536,32]{0,1:T(8,128)} %copy-done.20) | copy-start | bytes 589828
  572.3 3.6 copy-start.12
  572.3 3.6 copy-start.50
  576.0 2.7 copy-start.14
  579.8 3.5 copy-start.46
  579.8 3.5 copy-start.47
  585.3 3.5 copy-start.10
  585.3 3.5 copy-start.22
  585.3 3.5 copy-start.23
  588.9 4.0 copy-start.33
  599.6 2.5 copy-start.15
  599.6 3.6 copy-start.13
  602.1 2.7 copy-start.4
  604.9 3.0 copy-start.5
  607.9 3.0 copy-start.6
  629.9 106.4 %copy-start.36 = (pred[1760]{0:T(1024)(128)(4,1)S(1)}, pred[1760]{0:T(1024)(128)(4,1)}, u32[]{:S(2)}) copy-start(pred[1760]{0:T(1024)(128)(4,1)} %fusion.64) | copy-start | bytes 5284
  734.7 3.0 copy-start.16
  734.7 3.0 copy-start.17
  737.7 3.3 copy-start.18
  737.8 3.3 copy-start.27
  737.8 3.3 copy-start.28
  737.8 3.3 copy-start.29
  (9 other events, 12.6 us)
Sparse Core Ops, SparseCore 0:
  13.4 29.8 all-gather.4
  45.5 27.2 all-gather.2
  334.8 26.3 reduce-scatter.2
  557.9 26.3 reduce-scatter.4
  613.5 121.1 all-reduce.7

commit v2 on v1

v2 whole, which is shorter than its diff:
```python
import functools
import jax
import jax.numpy as jnp
from jax import lax
from jax.experimental import pallas as pl
from jax.experimental.pallas import tpu as pltpu
from jax.sharding import PartitionSpec as P

MESH = pl.DeviceIdType.MESH
bf16, f32 = jnp.bfloat16, jnp.float32
NN = (((1,), (0,)), ((), ()))
NT = (((1,), (1,)), ((), ()))
TN = (((0,), (0,)), ((), ()))
root_half = 0.7978845608028654


class Grid:
    def __init__(self, dp):
        half = dp // 2
        self.X = 1
        while self.X * self.X * 4 <= half:
            self.X *= 2
        self.planes = half // self.X
        self.devices = dp * 2
        self.swap = self.X == 2

    def here(self):
        return Grid(self.devices // 2).place()

    def place(self):
        dp = lax.axis_index("dp")
        self.core = lax.rem(dp, 2)
        self.x = lax.rem(lax.div(dp, 2), self.X)
        self.plane = lax.div(dp, 2 * self.X)
        self.y = lax.axis_index("group")
        self.flip = self.core if self.swap else 0
        if self.swap:
            self.a = jnp.where(self.core == 0, self.x, self.y)
            self.b = jnp.where(self.core == 0, self.y, self.x)
        else:
            self.a, self.b = self.x, self.y
        return self

    def xy(self, a, b):
        if not self.swap:
            return a, b
        return jnp.where(self.core == 0, a, b), jnp.where(self.core == 0, b, a)

    def device(self, plane=None, a=None, b=None, core=None):
        plane = self.plane if plane is None else plane
        a = self.a if a is None else a
        b = self.b if b is None else b
        x, y = self.xy(a, b)
        core = self.core if core is None else core
        return ((plane * self.X + x) * 2 + core, y)

    def index(self, plane, x, core, y):
        return ((plane * self.X + x) * 2 + core) * 2 + y

    def partners(self):
        found = [self.device(core=1 - self.core), self.device(b=1 - self.b)]
        found += [self.device(a=lax.rem(self.a + d, self.X)) for d in range(1, self.X)]
        found += [self.device(plane=lax.rem(self.plane + d, self.planes)) for d in range(1, self.planes)]
        return found


def enter(partners):
    barrier = pltpu.get_barrier_semaphore()
    for one in partners:
        pl.semaphore_signal(barrier, inc=1, device_id=one, device_id_type=MESH)
    pl.semaphore_wait(barrier, len(partners))


def add_rows(out, terms, rows, block):
    @pl.loop(0, rows // block)
    def _(step):
        part = pl.ds(pl.multiple_of(step * block, block), block)
        total = terms[0][part, :].astype(f32)
        for term in terms[1:]:
            total = total + term[part, :].astype(f32)
        out[part, :] = total.astype(out.dtype)


def block_of(rows):
    for tiles in range(12, 0, -1):
        if rows % (16 * tiles) == 0:
            return 16 * tiles


class Scatter:
    def __init__(self, grid, first, count, stride, window, base=0, pairs=0):
        self.g, self.first, self.count, self.stride, self.window = grid, first, count, stride, window
        self.base, self.pairs = base, pairs

    def scratch(self):
        g, n, w = self.g, self.count, self.window
        dma = pltpu.SemaphoreType.DMA
        return [
            pltpu.VMEM((n, g.X, 2, w, 128), bf16),
            pltpu.VMEM((n, g.X, 2, w, 128), bf16),
            pltpu.VMEM((n, g.X - 1, 2, w, 128), bf16),
            pltpu.VMEM((n, w, 128), bf16),
            dma((n, g.X, 2)), dma((n, g.X, 2)), dma((n, g.X, 2)),
            dma((n, g.X - 1, 2)), dma((n, g.X - 1, 2)),
            dma((n,)), dma((n,)), dma((n,)), dma((g.planes - 1,)),
        ]

    def shared(self):
        return [
            pltpu.VMEM((self.g.planes - 1, self.window, 128), bf16),
            pltpu.VMEM((self.window, 128), bf16),
        ]

    def bind(self, flat, out, scratch, shared):
        self.r4, self.kept = shared
        (self.own, self.r1, self.r2, self.r3, self.lsem, self.s1, self.q1, self.s2,
         self.q2, self.s3, self.q3, self.s4, self.q4) = scratch
        self.flat, self.out, self.g = flat, out, self.g.here()

    def plane_of(self, k):
        return self.first + lax.rem(self.g.plane + 1 + k, self.count)

    def copies0(self, k):
        g = self.g
        q = self.plane_of(k)
        for x in range(g.X):
            for y in range(2):
                there = pl.multiple_of(self.stride * g.index(q, x, 1 - g.core, y) - self.base, 16)
                here = pl.multiple_of(self.stride * g.index(q, x, g.core, y) - self.base, 16)
                yield (
                    pltpu.make_async_remote_copy(
                        self.flat.at[pl.ds(there, self.window), :], self.r1.at[k, x, y],
                        self.s1.at[k, x, y], self.q1.at[k, x, y],
                        device_id=g.device(core=1 - g.core), device_id_type=MESH),
                    pltpu.make_async_copy(
                        self.flat.at[pl.ds(here, self.window), :], self.own.at[k, x, y], self.lsem.at[k, x, y]),
                    x, y)

    def copies1(self, k):
        g = self.g
        for d in range(1, g.X):
            a = lax.rem(g.a + d, g.X)
            for b in range(2):
                x, y = g.xy(a, b)
                yield pltpu.make_async_remote_copy(
                    self.own.at[k, x, y], self.r2.at[k, d - 1, b], self.s2.at[k, d - 1, b], self.q2.at[k, d - 1, b],
                    device_id=g.device(a=a), device_id_type=MESH)

    def copy2(self, k):
        g = self.g
        x, y = g.xy(g.a, 1 - g.b)
        return pltpu.make_async_remote_copy(
            self.own.at[k, x, y], self.r3.at[k], self.s3.at[k], self.q3.at[k],
            device_id=g.device(b=1 - g.b), device_id_type=MESH)

    def copy3(self, k):
        g = self.g
        q = self.plane_of(k)
        slot = lax.rem(g.plane - q + g.planes, g.planes) - 1
        slot = jnp.maximum(slot, 0)
        return pltpu.make_async_remote_copy(
            self.own.at[k, g.x, g.y], self.r4.at[slot], self.s4.at[k], self.q4.at[slot],
            device_id=g.device(plane=q), device_id_type=MESH)

    def step(self, stage, k):
        g = self.g
        block = block_of(self.window)
        if stage == 0:
            for far, near, x, y in self.copies0(k):
                far.start()
                near.start()
        elif stage == 1:
            for far, near, x, y in self.copies0(k):
                near.wait()
                far.wait()
                add_rows(self.own.at[k, x, y], [self.own.at[k, x, y], self.r1.at[k, x, y]], self.window, block)
            for copy in self.copies1(k):
                copy.start()
        elif stage == 2:
            for copy in self.copies1(k):
                copy.wait()
            for b in range(2):
                x, y = g.xy(g.a, b)
                mine = self.own.at[k, x, y]
                add_rows(mine, [mine] + [self.r2.at[k, d, b] for d in range(g.X - 1)], self.window, block)
            self.copy2(k).start()
        elif stage == 3:
            self.copy2(k).wait()
            mine = self.own.at[k, g.x, g.y]
            q = self.plane_of(k)
            add_rows(mine, [mine, self.r3.at[k]], self.window, block)

            @pl.when(q != g.plane)
            def _():
                self.copy3(k).start()

            @pl.when(q == g.plane)
            def _():
                add_rows(self.kept, [mine], self.window, block)

    def finish(self):
        g = self.g
        for k in range(self.count):
            @pl.when(self.plane_of(k) != g.plane)
            def _():
                self.copy3(k).wait_send()

        inside = jnp.logical_and(g.plane >= self.first, g.plane < self.first + self.count)

        @pl.when(inside)
        def _():
            for d in range(g.planes - 1):
                pltpu.make_async_remote_copy(
                    self.kept, self.r4.at[d], self.s4.at[0], self.q4.at[d],
                    device_id=g.device(plane=lax.rem(g.plane + 1 + d, g.planes)), device_id_type=MESH).wait_recv()
            add_rows(self.out, [self.kept] + [self.r4.at[d] for d in range(g.planes - 1)], self.window,
                     block_of(self.window))

    def order(self):
        found = [(1, k) for k in range(self.count)]
        for t in range(self.count + 1):
            found += [(stage, k) for stage, k in ((2, t), (3, t - 1)) if 0 <= k < self.count]
        return found

    def all(self):
        for k in range(self.count):
            self.step(0, k)
        for stage, k in self.order():
            self.step(stage, k)
        self.finish()


def gather_kernel(grid, stride, fresh, tail, out, lsem, tsem, s0, q0, s1, q1, s2, q2, s3, q3):
    g = grid.here()
    enter(g.partners())
    X, planes = g.X, g.planes

    def rows(q, x, core, y):
        return out.at[pl.ds(pl.multiple_of(stride * g.index(q, x, core, y), 16), stride), :]

    mine = rows(g.plane, g.x, g.core, g.y)
    first = pltpu.make_async_copy(fresh, mine, lsem)
    first.start()
    rest = pltpu.make_async_copy(tail, out.at[pl.ds(stride * g.devices, g.devices), :], tsem)
    rest.start()

    def send0(d):
        return pltpu.make_async_remote_copy(
            fresh, mine, s0.at[d - 1], q0.at[d - 1],
            device_id=g.device(plane=lax.rem(g.plane + d, planes)), device_id_type=MESH)

    def plane_of(k):
        return lax.rem(g.plane - k + planes, planes)

    def send1(k):
        part = rows(plane_of(k), g.x, g.core, g.y)
        return pltpu.make_async_remote_copy(
            part, part, s1.at[k], q1.at[k], device_id=g.device(b=1 - g.b), device_id_type=MESH)

    def send2(k):
        for d in range(1, X):
            for b in range(2):
                x, y = g.xy(g.a, b)
                part = rows(plane_of(k), x, g.core, y)
                yield pltpu.make_async_remote_copy(
                    part, part, s2.at[k, d - 1, b], q2.at[k, d - 1, b],
                    device_id=g.device(a=lax.rem(g.a + d, X)), device_id_type=MESH)

    def send3(k):
        for x in range(X):
            for y in range(2):
                part = rows(plane_of(k), x, g.core, y)
                yield pltpu.make_async_remote_copy(
                    part, part, s3.at[k, x, y], q3.at[k, x, y],
                    device_id=g.device(core=1 - g.core), device_id_type=MESH)

    for d in range(1, planes):
        send0(d).start()
    first.wait()
    for t in range(planes + 2):
        if t < planes:
            if t > 0:
                send0(t).wait_recv()
            send1(t).start()
        k = t - 1
        if 0 <= k < planes:
            send1(k).wait_recv()
            for copy in send2(k):
                copy.start()
        k = t - 2
        if 0 <= k < planes:
            for copy in send2(k):
                copy.wait_recv()
            for copy in send3(k):
                copy.start()
    for k in range(planes):
        for copy in send3(k):
            copy.wait_recv()
    for d in range(1, planes):
        send0(d).wait_send()
    for k in range(planes):
        send1(k).wait_send()
        for copy in send2(k):
            copy.wait_send()
        for copy in send3(k):
            copy.wait_send()
    rest.wait()


def gather_rows(fresh, tail, grid, stride, collective_id):
    dma = pltpu.SemaphoreType.DMA
    n, X = grid.planes, grid.X
    total = (stride + 1) * grid.devices
    return pl.pallas_call(
        functools.partial(gather_kernel, grid, stride),
        out_shape=jax.ShapeDtypeStruct((total, 128), bf16),
        in_specs=[pl.BlockSpec(memory_space=pl.ANY)] * 2,
        out_specs=pl.BlockSpec(memory_space=pl.ANY),
        scratch_shapes=[dma, dma, dma((n - 1,)), dma((n - 1,)), dma((n,)), dma((n,)),
                        dma((n, X - 1, 2)), dma((n, X - 1, 2)), dma((n, X, 2)), dma((n, X, 2))],
        compiler_params=pltpu.CompilerParams(collective_id=collective_id, has_side_effects=True),
    )(fresh, tail)


def lane_mask(rows, head):
    lane = lax.broadcasted_iota(jnp.int32, (rows, 128), 1)
    return (lane < 64) if head == 0 else (lane >= 64)


far_steps = (8, 12, 16, 23, 32, 46, 64, 91)


def bucket_index(offset):
    distance = jnp.abs(offset)
    passed = sum((distance >= one).astype(jnp.int32) for one in far_steps)
    inside = jnp.where(distance < 8, distance, 7 + passed)
    return inside + 16 * (offset > 0).astype(jnp.int32)


def near_rows(table, rows, span, first_row):
    spans = rows // 128
    blocks = span // 128 + spans
    offset = (
        128 * (jnp.arange(blocks, dtype=jnp.int32)[:, None] - (spans - 1))
        - jnp.arange(128, dtype=jnp.int32)[None, :] - first_row)
    onehot = (bucket_index(offset)[None] == jnp.arange(table.shape[0], dtype=jnp.int32)[:, None, None])
    return jnp.sum(jnp.where(onehot[:, None], table.astype(f32)[:, :, None, None], 0.0), axis=0)


def dot_of(left, right, dims):
    return lax.dot_general(left, right, dims, preferred_element_type=f32)


def flatten_into(value, wide, out, first):
    rows, columns = value.shape
    parts = columns // 128
    for part in range(parts):
        wide[pl.ds(part, rows, stride=parts), :] = value[:, 128 * part : 128 * part + 128]
    size = rows * parts
    out[pl.ds(first, size), :] = wide[pl.ds(0, size), :].astype(bf16)


def ffn_kernel(steps, tall, bases, length, x_ref, mixed_ref, cot_ref, gain_ref, wo_ref, wg_ref, wu_ref, wd_ref,
               out_ref, ghid_ref, gmix_ref, ggain_ref, flat_ref,
               flat, wide, hidden, nf, nft, gout, gate_low, up_low, out_sum, gnf_sum, sems):
    step = pl.program_id(0)
    rows, width = x_ref.shape
    chunk = wg_ref.shape[1]
    o_base, g_base, u_base, d_base, end = bases
    parts = wg_ref.shape[0] // 128

    @pl.when(step == 0)
    def _():
        place = lax.broadcasted_iota(jnp.int32, (rows, width), 0) + lax.rem(lax.axis_index("dp"), 2) * rows
        cot = cot_ref[...]
        gout[...] = jnp.where(place < length[0:1, 0:1], cot, jnp.zeros_like(cot))
        total = x_ref[...].astype(f32) + dot_of(mixed_ref[...], wo_ref[...], NN)
        hidden[...] = total
        scale = lax.rsqrt(jnp.mean(total * total, axis=1, keepdims=True) + 1e-06)
        normed = (total * scale * gain_ref[...].astype(f32)).astype(bf16)
        nf[...] = normed
        nft[...] = normed.T
        out_sum[...] = total
        gnf_sum[...] = jnp.zeros_like(gnf_sum)
        flat[pl.ds(end, flat.shape[0] - end), :] = jnp.zeros((flat.shape[0] - end, 128), bf16)

    @pl.when(step < steps)
    def _():
        gate = dot_of(nf[...], wg_ref[...], NN)
        up = dot_of(nf[...], wu_ref[...], NN)
        ginner = dot_of(gout[...], wd_ref[...], NT)
        square = gate * gate
        th = jnp.tanh(root_half * (gate + 0.044715 * gate * square))
        half = 0.5 * (1.0 + th)
        act = gate * half
        slope = half + 0.5 * gate * (1.0 - th * th) * (root_half * (1.0 + 3 * 0.044715 * square))
        inner = (act * up).astype(bf16)
        ggate = (ginner * up * slope).astype(bf16)
        gup = (ginner * act).astype(bf16)
        gate_low[:, pl.ds(pl.multiple_of(step * chunk, chunk), chunk)] = ggate
        up_low[:, pl.ds(pl.multiple_of(step * chunk, chunk), chunk)] = gup
        out_sum[...] += dot_of(inner, wd_ref[...], NN)
        gnf_sum[...] += dot_of(ggate, wg_ref[...], NT) + dot_of(gup, wu_ref[...], NT)
        size = chunk * (width // 128)
        flatten_into(dot_of(inner, gout[...], TN), wide, flat, pl.multiple_of(d_base + step * size, 16))
        part = pl.ds(pl.multiple_of(d_base + step * size, 16), size)
        pltpu.make_async_copy(flat.at[part, :], flat_ref.at[part, :], sems.at[step]).start()

    @pl.when(step == steps - 1)
    def _():
        out_ref[...] = out_sum[...].astype(bf16)
        total = hidden[...]
        scale = lax.rsqrt(jnp.mean(total * total, axis=1, keepdims=True) + 1e-06)
        unit = total * scale
        grad = gnf_sum[...]
        ggain_ref[...] = jnp.sum(grad * unit, axis=0, keepdims=True)
        c2 = grad * gain_ref[...].astype(f32)
        ghid = gout[...].astype(f32) + scale * (c2 - unit * jnp.mean(c2 * unit, axis=1, keepdims=True))
        ghid_ref[...] = ghid
        branch = ghid.astype(bf16)
        gmix_ref[...] = dot_of(branch, wo_ref[...], NT).astype(bf16)
        size = width * width // 128
        flatten_into(dot_of(mixed_ref[...], branch, TN), wide, flat, o_base)
        part = pl.ds(o_base, size)
        pltpu.make_async_copy(flat.at[part, :], flat_ref.at[part, :], sems.at[steps]).start()

    turns = width // tall
    for k, (low, base) in enumerate(((gate_low, g_base), (up_low, u_base))):
        @pl.when(jnp.logical_and(step >= steps + k * turns, step < steps + (k + 1) * turns))
        def _():
            turn = step - steps - k * turns
            columns = low.shape[1]
            size = tall * columns // 128
            value = dot_of(nft[pl.ds(pl.multiple_of(turn * tall, tall), tall), :], low[...], NN)
            first = pl.multiple_of(base + turn * size, 16)
            flatten_into(value, wide, flat, first)
            pltpu.make_async_copy(flat.at[pl.ds(first, size), :], flat_ref.at[pl.ds(first, size), :], sems.at[step + 1]).start()

    @pl.when(step == steps + 2 * turns - 1)
    def _():
        rest = flat.shape[0] - end
        last = pltpu.make_async_copy(flat.at[pl.ds(end, rest), :], flat_ref.at[pl.ds(end, rest), :], sems.at[steps + 2 * turns + 1])
        last.start()
        for s in range(steps):
            size = chunk * (width // 128)
            part = pl.ds(d_base + s * size, size)
            pltpu.make_async_copy(flat.at[part, :], flat_ref.at[part, :], sems.at[s]).wait()
        part = pl.ds(o_base, width * width // 128)
        pltpu.make_async_copy(flat.at[part, :], flat_ref.at[part, :], sems.at[steps]).wait()
        for k, base in enumerate((g_base, u_base)):
            size = tall * gate_low.shape[1] // 128
            for turn in range(turns):
                part = pl.ds(base + turn * size, size)
                pltpu.make_async_copy(flat.at[part, :], flat_ref.at[part, :], sems.at[steps + k * turns + turn + 1]).wait()
        last.wait()


def ffn(length, x, mixed, cot, gain, wo, wg, wu, wd, pad_rows):
    rows, width = x.shape
    deep = wg.shape[1]
    chunk, tall = 256, 256
    steps = deep // chunk
    turns = width // tall
    square, oblong = width * width // 128, width * deep // 128
    bases = (0, square, square + oblong, square + 2 * oblong, square + 3 * oblong)
    total = bases[4] + pad_rows
    whole = lambda shape: pl.BlockSpec(shape, lambda s: (0, 0))
    at = lambda s: jnp.minimum(s, steps - 1)
    return pl.pallas_call(
        functools.partial(ffn_kernel, steps, tall, bases),
        grid=(steps + 2 * turns,),
        in_specs=[whole(length.shape), whole((rows, width)), whole((rows, width)), whole((rows, width)), whole((1, width)),
                  whole((width, width)),
                  pl.BlockSpec((width, chunk), lambda s: (0, at(s))),
                  pl.BlockSpec((width, chunk), lambda s: (0, at(s))),
                  pl.BlockSpec((chunk, width), lambda s: (at(s), 0))],
        out_specs=[whole((rows, width)), whole((rows, width)), whole((rows, width)), whole((1, width)),
                   pl.BlockSpec(memory_space=pl.ANY)],
        out_shape=[jax.ShapeDtypeStruct((rows, width), bf16), jax.ShapeDtypeStruct((rows, width), f32),
                   jax.ShapeDtypeStruct((rows, width), bf16), jax.ShapeDtypeStruct((1, width), f32),
                   jax.ShapeDtypeStruct((total, 128), bf16)],
        scratch_shapes=[
            pltpu.VMEM((total, 128), bf16), pltpu.VMEM((max(tall * deep, square * 128) // 128, 128), f32),
            pltpu.VMEM((rows, width), f32), pltpu.VMEM((rows, width), bf16), pltpu.VMEM((width, rows), bf16),
            pltpu.VMEM((rows, width), bf16), pltpu.VMEM((rows, deep), bf16), pltpu.VMEM((rows, deep), bf16),
            pltpu.VMEM((rows, width), f32), pltpu.VMEM((rows, width), f32),
            pltpu.SemaphoreType.DMA((steps + 2 * turns + 2,))],
        compiler_params=pltpu.CompilerParams(vmem_limit_bytes=56 << 20),
    )(length, x, mixed, cot, gain, wo, wg, wu, wd)


def near_toeplitz(y_ref, head, b):
    near = jnp.concatenate([y_ref[head, b : b + 1, :], y_ref[head, b + 1 : b + 2, :]], axis=1)
    return pltpu.roll(jnp.broadcast_to(near, (128, 256)), 0, 1, stride=1, stride_axis=0)[:, :128]


def front_kernel(grid, chunk, tok_ref, cot_ref, len_ref, gain_ref, wq_ref, wk_ref, wv_ref, y_ref,
                 x_out, cot_out, len_out, normed_out, q_out, k_out, v_out, mixed_out, prob_ref,
                 xs, cs, ls, keys, values, bias, score, sems, s_kv, r_kv):
    g = grid.here()
    pair = pl.program_id(0)
    rows, width = tok_ref.shape
    span = keys.shape[0]
    spans = rows // 128
    blocks = span // 128 + spans - 1
    mate = g.device(core=1 - g.core)
    dp = lax.axis_index("dp")
    twin = (dp - g.core + g.y, g.core)
    moved = g.core != g.y
    first = pl.multiple_of(g.core * rows, rows)

    def move(k, begin):
        src, dst = ((tok_ref, xs), (cot_ref, cs))[k]

        @pl.when(moved)
        def _():
            far = pltpu.make_async_remote_copy(
                src, dst, sems.at[2 * k], sems.at[2 * k + 1], device_id=twin, device_id_type=MESH)
            far.start() if begin else far.wait()

        @pl.when(jnp.logical_not(moved))
        def _():
            near = pltpu.make_async_copy(src, dst, sems.at[2 * k + 1])
            near.start() if begin else near.wait()

    lens_copy = lambda: pltpu.make_async_remote_copy(len_ref, ls, sems.at[4], sems.at[5], device_id=mate, device_id_type=MESH)

    def swaps():
        part = pl.ds(first, rows)
        for k, buf in enumerate((keys, values)):
            yield pltpu.make_async_remote_copy(buf.at[part, :], buf.at[part, :], s_kv.at[k], r_kv.at[k], device_id=mate, device_id_type=MESH)

    @pl.when(pair == 0)
    def _():
        barrier = pltpu.get_barrier_semaphore()
        pl.semaphore_signal(barrier, inc=1, device_id=mate, device_id_type=MESH)

        @pl.when(moved)
        def _():
            pl.semaphore_signal(barrier, inc=1, device_id=twin, device_id_type=MESH)

        pl.semaphore_wait(barrier, jnp.where(moved, 2, 1))
        move(0, True)
        move(1, True)
        lens = lens_copy()
        lens.start()
        move(0, False)
        wide = xs[...].astype(f32)
        normed = (wide * lax.rsqrt(jnp.mean(wide * wide, axis=1, keepdims=True) + 1e-06)
                  * gain_ref[...].astype(f32)).astype(bf16)
        x_out[...] = xs[...]
        normed_out[...] = normed
        keys[pl.ds(first, rows), :] = dot_of(normed, wk_ref[...], NN).astype(bf16)
        values[pl.ds(first, rows), :] = dot_of(normed, wv_ref[...], NN).astype(bf16)
        for copy in swaps():
            copy.start()
        q_out[...] = dot_of(normed, wq_ref[...], NN).astype(bf16)
        lens.wait()
        len_out[...] = jnp.where(moved, ls[...], len_ref[...])
        for copy in swaps():
            copy.wait()

    lanes = pl.ds(pl.multiple_of(128 * pair, 128), 128)
    live = len_out[0:1, 0:1]
    for head in range(2):
        for b in range(blocks):
            bias[head, pl.ds(128 * b, 128), :] = near_toeplitz(y_ref, head, b)
    halves = []
    for head in range(2):
        query = q_out[:, lanes]
        query = jnp.where(lane_mask(rows, head), query, jnp.zeros_like(query))
        top = jnp.full((1, rows), -jnp.inf, f32)
        for c in range(span // chunk):
            part = pl.ds(chunk * c, chunk)
            raw = dot_of(keys[part, lanes], query, NT)
            added = jnp.concatenate(
                [bias[head, pl.ds(128 * (spans - 1 - s) + chunk * c, chunk), :] for s in range(spans)], axis=1)
            place = lax.broadcasted_iota(jnp.int32, (chunk, rows), 0) + chunk * c
            raw = jnp.where(place < live, raw + added, -jnp.inf)
            score[head, part, :] = raw
            top = jnp.maximum(top, jnp.max(raw, axis=0, keepdims=True))
        total = jnp.zeros((1, rows), f32)
        for c in range(span // chunk):
            part = pl.ds(chunk * c, chunk)
            grown = jnp.exp(score[head, part, :] - top)
            score[head, part, :] = grown
            total = total + jnp.sum(grown, axis=0, keepdims=True)
        inverse = 1.0 / total
        for c in range(span // chunk):
            part = pl.ds(chunk * c, chunk)
            prob_ref[head, part, :] = (score[head, part, :] * inverse).astype(bf16)
        halves.append(dot_of(values[:, lanes], prob_ref[head], TN))
    both = jnp.concatenate([halves[0][:64], halves[1][64:]], axis=0)
    mixed_out[:, lanes] = both.T.astype(bf16)

    @pl.when(pair == pl.num_programs(0) - 1)
    def _():
        k_out[...] = keys[...]
        v_out[...] = values[...]
        move(1, False)
        cot_out[...] = cs[...]


def once(shape):
    return pl.BlockSpec(shape, lambda s: (0,) * len(shape), pipeline_mode=pl.Buffered(1))


def front(grid, tokens, cot, lens, gain, wq, wk, wv, near, collective_id):
    rows, width = tokens.shape
    span, pairs, blocks = 2 * rows, width // 128, near.shape[1]
    row_shape, key_shape = (rows, width), (span, width)
    dma = pltpu.SemaphoreType.DMA
    return pl.pallas_call(
        functools.partial(front_kernel, grid, 256),
        grid=(pairs,),
        in_specs=[once(row_shape), once(row_shape), once(lens.shape), once((1, width)),
                  once((width, width)), once((width, width)), once((width, width)),
                  pl.BlockSpec((2, blocks, 128), lambda p: (p, 0, 0))],
        out_specs=[once(row_shape), once(row_shape), once(lens.shape), once(row_shape), once(row_shape),
                   once(key_shape), once(key_shape), once(row_shape),
                   pl.BlockSpec((2, span, rows), lambda p: (p, 0, 0))],
        out_shape=[jax.ShapeDtypeStruct(s, t) for s, t in (
            (row_shape, bf16), (row_shape, bf16), (lens.shape, jnp.int32), (row_shape, bf16), (row_shape, bf16),
            (key_shape, bf16), (key_shape, bf16), (row_shape, bf16), ((2 * pairs, span, rows), bf16))],
        scratch_shapes=[pltpu.VMEM(row_shape, bf16), pltpu.VMEM(row_shape, bf16), pltpu.VMEM(lens.shape, jnp.int32),
                        pltpu.VMEM(key_shape, bf16), pltpu.VMEM(key_shape, bf16),
                        pltpu.VMEM((2, 128 * (blocks - 1), 128), f32), pltpu.VMEM((2, span, rows), f32),
                        dma((6,)), dma((2,)), dma((2,))],
        compiler_params=pltpu.CompilerParams(collective_id=collective_id, has_side_effects=True, vmem_limit_bytes=56 << 20),
    )(tokens, cot, lens, gain, wq, wk, wv, near)


class TailSum:
    def __init__(self, grid, rows):
        self.g, self.rows = grid, rows
        self.sizes = (2, grid.X, 2, grid.planes)

    def scratch(self):
        dma = pltpu.SemaphoreType.DMA
        return [pltpu.VMEM((size, self.rows, 128), f32) for size in self.sizes] + [
            dma((sum(self.sizes),)), dma((sum(self.sizes),))]

    def bind(self, scratch):
        self.bufs, self.send, self.recv = scratch[:4], scratch[4], scratch[5]
        self.g = g = self.g.here()
        self.places = (g.core, g.a, g.b, g.plane)

    def mate(self, axis, place):
        g = self.g
        return (g.device(core=place), g.device(a=place), g.device(b=place), g.device(plane=place))[axis]

    def mine(self, axis):
        return self.bufs[axis].at[self.places[axis]]

    def copies(self, axis):
        base = sum(self.sizes[:axis])
        for d in range(1, self.sizes[axis]):
            there = lax.rem(self.places[axis] + d, self.sizes[axis])
            buf = self.bufs[axis]
            yield pltpu.make_async_remote_copy(
                buf.at[self.places[axis]], buf.at[self.places[axis]], self.send.at[base + d], self.recv.at[base + d],
                device_id=self.mate(axis, there), device_id_type=MESH)

    def start(self, axis):
        for copy in self.copies(axis):
            copy.start()

    def done(self, axis):
        for copy in self.copies(axis):
            copy.wait_send()
        base = sum(self.sizes[:axis])
        for d in range(1, self.sizes[axis]):
            behind = lax.rem(self.places[axis] - d + self.sizes[axis], self.sizes[axis])
            buf = self.bufs[axis]
            pltpu.make_async_remote_copy(
                buf.at[behind], buf.at[behind], self.send.at[base + d], self.recv.at[base + d],
                device_id=self.mate(axis, behind), device_id_type=MESH).wait_recv()
        total = self.bufs[axis][0]
        for k in range(1, self.sizes[axis]):
            total = total + self.bufs[axis][k]
        return total


def adam_step(grads, moment_one, moment_two, master):
    moment_one_new = 0.9 * moment_one + 0.1 * grads
    moment_two_new = 0.999 * moment_two + 0.001 * grads * grads
    first_hat = moment_one_new / (1.0 - 0.9**10)
    second_hat = moment_two_new / (1.0 - 0.999**10)
    master_new = master - 0.01 * (first_hat / (jnp.sqrt(second_hat) + 1e-08) + 0.1 * master)
    return moment_one_new, moment_two_new, master_new


def dot_exact(left, right):
    return lax.dot_general(left, right, NN, precision=lax.Precision.HIGHEST, preferred_element_type=f32)


def diagonals(block):
    row = lax.broadcasted_iota(jnp.int32, (128, 128), 0)
    lane = lax.broadcasted_iota(jnp.int32, (128, 128), 1)
    turned = dot_exact(block, (row + lane == 127).astype(f32))
    wide = jnp.concatenate([turned, jnp.zeros_like(turned)], axis=1)
    return jnp.sum(pltpu.roll(wide, 0, 1, stride=1, stride_axis=0), axis=0, keepdims=True)


def table_rows(diag, far, heads, buckets):
    tall = diag.shape[1]
    lane = lax.broadcasted_iota(jnp.int32, (tall, 128), 1)
    sums = jnp.where(lane == buckets // 2 - 1, jnp.sum(far[0], axis=1, keepdims=True), 0.0)
    sums = sums + jnp.where(lane == buckets - 1, jnp.sum(far[1], axis=1, keepdims=True), 0.0)
    for n in range(3):
        offset = lax.broadcasted_iota(jnp.int32, (256, 128), 0) - 127 + 128 * (n - 1)
        onehot = bucket_index(offset) == lax.broadcasted_iota(jnp.int32, (256, 128), 1)
        sums = sums + dot_exact(diag[n], onehot.astype(f32))
    found = []
    for t in range(heads * buckets // 128):
        place = lax.broadcasted_iota(jnp.int32, (128, 128), 1) + 128 * t
        bucket = lax.broadcasted_iota(jnp.int32, (128, 128), 0)
        spread = jnp.logical_and(place >= heads * bucket, place < heads * bucket + heads)
        wide = dot_exact(sums, spread.astype(f32))
        place = lax.broadcasted_iota(jnp.int32, (tall, 128), 1) + 128 * t
        head = place - heads * ((place * (65536 // heads + 1)) >> 16)
        mine = head == lax.broadcasted_iota(jnp.int32, (tall, 128), 0)
        found.append(jnp.sum(jnp.where(mine, wide, 0.0), axis=0, keepdims=True))
    return found


def back_kernel(grid, chunk, early, late, ends, heads, buckets, *refs):
    (q_ref, k_ref, v_ref, gm_ref, mixed_ref, prob_ref, normed_ref, x_ref, ghid_ref, gain_ref, wq_ref, wk_ref, wv_ref,
     lo_ref, ggain_ref, m1_ref, m2_ref, ma_ref, flat_ref,
     lo_out, gtok_out, gshard_out, m1_out, m2_out, ma_out, fresh_out, ftail_out) = refs[:27]
    rest = refs[27:]
    taken = []
    for job in (early, late, ends):
        size = len(job.scratch())
        taken.append(rest[:size])
        rest = rest[size:]
    shared, rest = rest[:2], rest[2:]
    (slope, gq, gk, gv, rk, rv, flat, wide, diag, far, lo_in, gt_in, halo, halo_in, summed, renewed,
     lsem, s_kv, r_kv, s_turn, r_turn) = rest
    g = grid.here()
    step = pl.program_id(0)
    rows, width = normed_ref.shape
    keys = k_ref.shape[0]
    spans = rows // 128
    blocks = keys // 128 + spans - 1
    pairs = pl.num_programs(0) - 1
    first = spans - 1 + g.core * spans
    mate = g.device(core=1 - g.core)
    dp = lax.axis_index("dp")
    twin = (dp - g.core + g.y, g.core)
    moved = g.core != g.y
    count = grid.devices
    place = dp * 2 + g.y
    after = lax.rem(place + 1, count)
    nextdoor = (lax.div(after, 2), lax.rem(after, 2))
    before = lax.rem(place + count - 1, count)
    prior = (lax.div(before, 2), lax.rem(before, 2))
    shard = ma_ref.shape[0]
    stride, window = early.stride, early.window
    early.bind(flat_ref, summed.at[pl.ds(count, window), :], taken[0], shared)
    late.bind(flat, summed.at[pl.ds(count, window), :], taken[1], shared)
    ends.bind(taken[2])
    order = early.order()
    square = width * width // 128
    over = flat.shape[0] - 3 * square
    edge = lambda: pltpu.make_async_copy(flat_ref.at[pl.ds(0, over), :], flat.at[pl.ds(3 * square, over), :], lsem.at[0])
    lo_copy = lambda: pltpu.make_async_remote_copy(
        lo_ref, lo_in, s_turn.at[0], r_turn.at[0], device_id=twin, device_id_type=MESH)
    ghid_copy = lambda: pltpu.make_async_copy(ghid_ref, gtok_out, lsem.at[1])
    lo_stay = lambda: pltpu.make_async_copy(lo_ref, lo_in, r_turn.at[0])
    gt_copy = lambda: pltpu.make_async_remote_copy(
        gq, gt_in, s_turn.at[1], r_turn.at[1], device_id=twin, device_id_type=MESH)
    halo_copy = lambda: pltpu.make_async_remote_copy(
        halo, halo_in, s_turn.at[2], r_turn.at[2], device_id=nextdoor, device_id_type=MESH)

    def square_grad(right, base):
        half = width // 2
        for k in range(2):
            flatten_into(dot_of(normed_ref[:, half * k : half * k + half], right, TN), wide, flat, base + k * square // 2)

    @pl.when(step == 0)
    def _():
        barrier = pltpu.get_barrier_semaphore()
        partners = g.partners() + [prior, nextdoor]
        for one in partners:
            pl.semaphore_signal(barrier, inc=1, device_id=one, device_id_type=MESH)

        @pl.when(moved)
        def _():
            pl.semaphore_signal(barrier, inc=1, device_id=twin, device_id_type=MESH)

        pl.semaphore_wait(barrier, len(partners) + jnp.where(moved, 1, 0))
        edge().start()
        ghid_copy().start()
        for k in range(early.count):
            early.step(0, k)
        for k, state in enumerate((m1_ref, m2_ref, ma_ref)):
            halo[k] = state[pl.ds(shard - count, count), :]
        halo_copy().start()

        @pl.when(moved)
        def _():
            lo_copy().start()

        @pl.when(jnp.logical_not(moved))
        def _():
            lo_stay().start()

    for n, (stage, k) in enumerate(order):
        if n + 1 < late.pairs:
            @pl.when(step == n + 1)
            def _():
                early.step(stage, k)

    @pl.when(step < pairs)
    def _():
        inner = (gm_ref[...].astype(f32) * mixed_ref[...].astype(f32)).T
        parts = ([], [], [])
        for head in range(2):
            row_inner = jnp.sum(inner[64 * head : 64 * head + 64], axis=0, keepdims=True)
            grown = gm_ref[...]
            grown = jnp.where(lane_mask(rows, head), grown, jnp.zeros_like(grown))
            for c in range(keys // chunk):
                part = pl.ds(chunk * c, chunk)
                back = dot_of(v_ref[part, :], grown, NT)
                slope[head, part, :] = (prob_ref[head, part, :].astype(f32) * (back - row_inner)).astype(bf16)
            parts[0].append(dot_of(k_ref[...], slope[head], TN))
            parts[1].append(dot_of(slope[head], q_ref[...], NN))
            parts[2].append(dot_of(prob_ref[head], gm_ref[...], NN))
            low = jnp.zeros((8, 128), f32)
            high = jnp.zeros((8, 128), f32)
            mids = [jnp.zeros((128, 128), f32) for _ in range(3)]
            for b in range(blocks):
                total = None
                for s in range(spans):
                    j = b - (spans - 1) + s
                    if 0 <= j < keys // 128:
                        term = slope[head, pl.ds(128 * j, 128), pl.ds(128 * s, 128)].astype(f32)
                        total = term if total is None else total + term
                wide[pl.ds(128 * b, 128), :] = total
                folded = total.reshape(16, 8, 128).sum(axis=0)
                low = low + jnp.where(b < first - 1, folded, 0.0)
                high = high + jnp.where(b > first + 1, folded, 0.0)
            line = pl.ds(2 * step + head, 1)
            for n in range(3):
                near = wide[pl.ds(pl.multiple_of(128 * (first - 1 + n), 128), 128), :]
                diag[n, line, :] = diagonals(near)
            far[0, line, :] = jnp.sum(low, axis=0, keepdims=True)
            far[1, line, :] = jnp.sum(high, axis=0, keepdims=True)
        lanes = pl.ds(pl.multiple_of(128 * step, 128), 128)
        gq[:, lanes] = jnp.concatenate([parts[0][0][:64], parts[0][1][64:]], axis=0).T.astype(bf16)
        mask = lane_mask(keys, 0)
        gk[:, lanes] = jnp.where(mask, parts[1][0], parts[1][1]).astype(bf16)
        gv[:, lanes] = jnp.where(mask, parts[2][0], parts[2][1]).astype(bf16)

    @pl.when(step == pairs)
    def _():
        mine = pl.ds(pl.multiple_of(g.core * rows, rows), rows)
        other = pl.ds(pl.multiple_of((1 - g.core) * rows, rows), rows)
        copies = [pltpu.make_async_remote_copy(a.at[other, :], b, s_kv.at[k], r_kv.at[k], device_id=mate, device_id_type=MESH)
                  for k, (a, b) in enumerate(((gk, rk), (gv, rv)))]
        for copy in copies:
            copy.start()
        square_grad(gq[...], 0)
        total = dot_of(gq[...], wq_ref[...], NT)
        for k, (a, b, w) in enumerate(((gk, rk, wk_ref), (gv, rv, wv_ref))):
            copies[k].wait()
            low = (a[mine, :].astype(f32) + b[...].astype(f32)).astype(bf16)
            b[...] = low
            square_grad(low, (k + 1) * square)
            total = total + dot_of(low, w[...], NT)
        edge().wait()
        for k in range(late.count):
            late.step(0, k)
        x = x_ref[...].astype(f32)
        scale = lax.rsqrt(jnp.mean(x * x, axis=1, keepdims=True) + 1e-06)
        unit = x * scale
        gain_row = jnp.sum(total * unit, axis=0, keepdims=True)
        c1 = total * gain_ref[...].astype(f32)
        ghid_copy().wait()
        gtok = gtok_out[...] + scale * (c1 - unit * jnp.mean(c1 * unit, axis=1, keepdims=True))
        gtok_out[...] = gtok

        @pl.when(moved)
        def _():
            gq[...] = gtok.astype(bf16)
            gt_copy().start()

        tail = ends.mine(0)
        tail[...] = jnp.zeros(tail.shape, f32)
        for r in range(width // 128):
            tail[r : r + 1, :] = gain_row[:, 128 * r : 128 * r + 128]
            tail[width // 128 + r : width // 128 + r + 1, :] = ggain_ref[:, 128 * r : 128 * r + 128]
        for r, line in enumerate(table_rows(diag, far, heads, buckets)):
            tail[2 * width // 128 + r : 2 * width // 128 + r + 1, :] = line
        for k in range(3):
            tail[16 + k * count : 16 + (k + 1) * count, :] = jnp.where(place == count - 1, halo[k], 0.0)
        ends.start(0)

        left = [(early, stage, k) for n, (stage, k) in enumerate(order) if n + 1 >= late.pairs]
        left += [(late, stage, k) for stage, k in late.order()]
        for n, (job, stage, k) in enumerate(left):
            job.step(stage, k)
            if n < 3:
                found = ends.done(n)
                ends.mine(n + 1)[...] = found
                ends.start(n + 1)
        found = ends.done(3)
        summed[pl.ds(0, count), :] = jnp.zeros((count, 128), f32)
        early.finish()
        late.finish()

        @pl.when(place == count - 1)
        def _():
            summed[pl.ds(count + stride, count), :] = jnp.zeros((count, 128), f32)
            summed[pl.ds(count + stride, 16), :] = found[:16]

        grads = jnp.concatenate([found[:16], jnp.zeros((count - 16, 128), f32)], axis=0)
        last = [found[16 + k * count : 16 + (k + 1) * count] for k in range(3)]
        ftail_out[...] = adam_step(grads, *last)[2].astype(bf16)
        halo_copy().wait()
        renewed[pl.ds(0, count), :] = adam_step(summed[pl.ds(place, count), :], *[halo_in[k] for k in range(3)])[2]
        for start in range(0, shard, 216):
            size = min(216, shard - start)
            part = pl.ds(start, size)
            grads = summed[pl.ds(place + count + start, size), :]
            one, two, new = adam_step(grads, m1_ref[part, :], m2_ref[part, :], ma_ref[part, :])
            gshard_out[part, :] = grads
            m1_out[part, :] = one
            m2_out[part, :] = two
            ma_out[part, :] = new
            renewed[pl.ds(count + start, size), :] = new
        for start in range(0, stride, stride // 8):
            fresh_out[pl.ds(start, stride // 8), :] = renewed[pl.ds(start + count - place, stride // 8), :].astype(bf16)

        @pl.when(moved)
        def _():
            lo_copy().wait()
            gt_copy().wait()
            gtok_out[...] = gt_in[...].astype(f32)

        @pl.when(jnp.logical_not(moved))
        def _():
            lo_stay().wait()

        lo_out[...] = lo_in[...]


def back(grid, heads, buckets, query, keys_all, values_all, grad_mixed, mixed, prob, normed, x, grad_hidden, gain,
         wq, wk, wv, layer_out, ggain, moment_one, moment_two, master, flat, collective_id):
    rows, width = query.shape
    span = keys_all.shape[0]
    pairs = width // 128
    shard = master.shape[0]
    count = grid.devices
    stride, window = shard - 1, shard - 1 + count
    cut = grid.planes // 4
    late_rows = 3 * width * width // 128
    early = Scatter(grid, cut, grid.planes - cut, stride, window, late_rows, pairs)
    late = Scatter(grid, 0, cut, stride, window, 0, pairs)
    ends = TailSum(grid, 16 + 3 * count)
    at = lambda s: jnp.minimum(s, pairs - 1)
    tall = lambda n: pl.BlockSpec((n, 128), lambda s: (0, at(s)))
    dma = pltpu.SemaphoreType.DMA
    state = (shard, 128)
    return pl.pallas_call(
        functools.partial(back_kernel, grid, 256, early, late, ends, heads, buckets),
        grid=(pairs + 1,),
        in_specs=[tall(rows), tall(span), tall(span), tall(rows), tall(rows),
                  pl.BlockSpec((2, span, rows), lambda s: (at(s), 0, 0)),
                  once((rows, width)), once((rows, width)), pl.BlockSpec(memory_space=pl.ANY), once((1, width)),
                  once((width, width)), once((width, width)), once((width, width)),
                  pl.BlockSpec(memory_space=pl.ANY), once((1, width)), once(state), once(state), once(state),
                  pl.BlockSpec(memory_space=pl.ANY)],
        out_specs=[once((rows, width)), once((rows, width)), once(state), once(state), once(state), once(state),
                   once((stride, 128)), once((count, 128))],
        out_shape=[jax.ShapeDtypeStruct(s, t) for s, t in (
            ((rows, width), bf16), ((rows, width), f32), (state, f32), (state, f32), (state, f32), (state, f32),
            ((stride, 128), bf16), ((count, 128), bf16))],
        scratch_shapes=early.scratch() + late.scratch() + ends.scratch() + early.shared() + [
            pltpu.VMEM((2, span, rows), bf16), pltpu.VMEM((rows, width), bf16),
            pltpu.VMEM((span, width), bf16), pltpu.VMEM((span, width), bf16),
            pltpu.VMEM((rows, width), bf16), pltpu.VMEM((rows, width), bf16),
            pltpu.VMEM((late_rows + count, 128), bf16), pltpu.VMEM((late_rows // 6, 128), f32),
            pltpu.VMEM((3, 16, 256), f32), pltpu.VMEM((2, 16, 128), f32),
            pltpu.VMEM((rows, width), bf16), pltpu.VMEM((rows, width), bf16),
            pltpu.VMEM((3, count, 128), f32), pltpu.VMEM((3, count, 128), f32),
            pltpu.VMEM((count + window, 128), f32), pltpu.VMEM((count + shard + 7, 128), f32),
            dma((2,)), dma((2,)), dma((2,)), dma((3,)), dma((3,))],
        compiler_params=pltpu.CompilerParams(collective_id=collective_id, has_side_effects=True, vmem_limit_bytes=62 << 20),
    )(query, keys_all, values_all, grad_mixed, mixed, prob, normed, x, grad_hidden, gain, wq, wk, wv, layer_out, ggain,
      moment_one, moment_two, master, flat)


def per_device(tokens, lengths, cotangent, w_query, w_keys, w_values, w_output, w_gate, w_up, w_down,
               gain_attn, gain_ffn, bias_table, master, moment_one, moment_two):
    rows, width = tokens.shape
    grid = Grid(lax.axis_size("dp")).here()
    span = rows * lax.axis_size("group")
    count = grid.devices
    first_row = grid.core * rows
    near = near_rows(bias_table, rows, span, first_row)
    lens = jnp.broadcast_to(lengths.reshape(1, 1), (8, 128))
    gain_one, gain_two = gain_attn.reshape(1, width), gain_ffn.reshape(1, width)
    x, cot, lens, normed, query, keys_all, values_all, mixed, prob = front(
        grid, tokens, cotangent, lens, gain_one, w_query, w_keys, w_values, near, 1)
    layer_out, grad_hidden, grad_mixed, grad_gain_ffn, flat = ffn(
        lens, x, mixed, cot, gain_two, w_output, w_gate, w_up, w_down, count)
    layer_out, grad_tokens, grad_shard, moment_one_new, moment_two_new, master_new, fresh, fresh_tail = back(
        grid, bias_table.shape[1], bias_table.shape[0], query, keys_all, values_all, grad_mixed, mixed, prob, normed, x,
        grad_hidden, gain_one, w_query, w_keys, w_values, layer_out, grad_gain_ffn, moment_one, moment_two, master, flat, 2)
    fresh_copy = gather_rows(fresh, fresh_tail, grid, master.shape[0] - 1, 3)
    return (layer_out, grad_tokens, grad_shard, moment_one_new, moment_two_new, master_new, fresh_copy)


def solution(mesh):
    both = P(("dp", "group"), None)
    return jax.shard_map(
        per_device,
        mesh=mesh,
        in_specs=(both, P("dp"), both) + (P(),) * 10 + (both,) * 3,
        out_specs=(both,) * 6 + (P(),),
        check_vma=False,
    )
```

time: 858 us -> 312 us (0.36); the launches traced: 844 us -> 308 us
  local copies, waits for them, and re-layouts: 414 us -> 22.4 us
  matrix products: 138 us -> 0 us
  Pallas kernels: 164 us -> 283 us
  other arithmetic: 87 us -> 1.9 us
  waiting for transfers between devices: 23.1 us -> 0 us
  between operations: 15.2 us -> 1.37 us
    reshape x10 -> x2, local copies, waits for them, and re-layouts: 168 us -> 2.53 us  [the longest x1 1.26 us: per_device(): gain_attn.reshape(1, width)]
    dot_general x27 -> x0, matrix products: 138 us -> none  [the longest x7 28.5 us: product_tn(): lax.dot_general(left_op, right_op, (((0,), (0,)), ((), ())), preferred_el...]
    unnamed x112 -> x19, local copies, waits for them, and re-layouts: 157 us -> 19.3 us
    pallas_call x1 -> x3, Pallas kernels: 81.9 us -> 203 us  [the longest x1 134 us: back(): pl.pallas_call(functools.partial(back_kernel, grid, 256, early, late, end...]
    convert_element_type x9 -> x1, other arithmetic: 48.7 us -> 0.69 us  [near_rows(): table.astype(f32)[:, :, None, None]]
    slice x1 -> x0, local copies, waits for them, and re-layouts: 37.7 us -> none  [skew_bias(): lax.slice_in_dim(repeated, block_rows - 1, block_rows - 1 + block_rows *...]
    reduce_sum x6 -> x1, other arithmetic: 27.1 us -> 1.09 us  [near_rows(): jnp.sum(jnp.where(onehot[:, None], table.astype(f32)[:, :, None, None], 0...]
    pad x2 -> x0, local copies, waits for them, and re-layouts: 24.8 us -> none  [the longest x1 12.8 us: per_device(): flat = jnp.pad(flat, ((0, count), (0, 0)))]
  transfers between devices with their start and end apart: 6 -> 0, of which waited for: 1 -> 0; matrix products, arithmetic and copies ran while one was open for 60% -> 0% of each run, Pallas kernels for 10% -> 0%
where the time goes in v2:
time: 312 us; the launch traced here: 308 us
  Pallas kernels  283 us (91%)
  local copies, waits for them, and re-layouts  22.4 us (7%)
    pallas_call x1, Pallas kernels, back(): pl.pallas_call(functools.partial(back_kernel, grid, 256, early, late, end...  134 us
    pallas_call x1, Pallas kernels, gather_rows(): pl.pallas_call(functools.partial(gather_kernel, grid, stride), out_shape=...  79.3 us
    pallas_call x1, Pallas kernels, front(): pl.pallas_call(functools.partial(front_kernel, grid, 256), grid=(pairs,),...  39.9 us
    pallas_call x1, Pallas kernels, ffn(): pl.pallas_call(functools.partial(ffn_kernel, steps, tall, bases), grid=(s...  29.5 us
    unnamed x19, local copies, waits for them, and re-layouts  19.3 us

profile of v2, /device:TPU:0, one launch (start us, length us, event | category | flops | bytes accessed | tf_op | source)
XLA Modules:
  0.0 308.4 jit_solution(5679535011430811359)
XLA Ops:
  1.3 1.3 reshape.83.gain_ref.refs_9_
  2.6 1.3 reshape.84.gain_ref
  3.8 0.6 broadcast_in_dim.34.len_ref
  4.4 0.1 fusion
  4.5 0.7 convert_element_type.68
  5.2 1.1 select_reduce_fusion.y_ref
  6.3 39.9 %shard_map.207 = (bf16[512,768]{1,0:T(8,128)(2,1)}, bf16[512,768]{1,0:T(8,128)(2,1)}, s32[8,128]{1,0:T(8,128)}, bf16[512,768]{1,0:T(8,128)(2,1)}, bf16[512,768]{...) custom-call(bf16[512,768]{1,0:T(8,128)(2,1)} %tok_ref.1, ...), custom_call_target="tpu_custom_call" | custom-call | tf_op jit(solution)/shard_map/pallas_call | solution.py:613
  46.2 29.5 %shard_map.208 = (bf16[512,768]{1,0:T(8,128)(2,1)}, f32[512,768]{1,0:T(8,128)}, bf16[512,768]{1,0:T(8,128)(2,1)}, f32[1,768]{1,0:T(1,128)}, bf16[41504,128]{1,0:T(8,128)(2,1)}) custom-call(s32[8,128]{1,0:T(8,128)} %get-tuple-element.32.length, bf16[512,768]{1,0:T(8,128)(2,1)} %get-tuple-element.33.x_ref.refs_7_, ...), custom_call_target="tpu_custom_call" | custom-call | tf_op jit(solution)/shard_map/pallas_call | solution.py:469
  75.7 134.1 %shard_map.209 = (bf16[512,768]{1,0:T(8,128)(2,1)}, f32[512,768]{1,0:T(8,128)}, f32[1729,128]{1,0:T(8,128)}, f32[1729,128]{1,0:T(8,128)}, f32[1729,128]{1,0:T(8,...) custom-call(bf16[512,768]{1,0:T(8,128)(2,1)} %get-tuple-element.29.refs_0_, ...), custom_call_target="tpu_custom_call" | custom-call | tf_op jit(solution)/shard_map/pallas_call | solution.py:966
  209.8 0.0 copy-start.5
  209.8 79.3 %shard_map.210 = bf16[55328,128]{1,0:T(8,128)(2,1)} custom-call(bf16[1728,128]{1,0:T(8,128)(2,1)} %get-tuple-element.49.fresh, bf16[32,128]{1,0:T(8,128)(2,1)} %get-tuple-element.50.tail), custom_call_target="tpu_custom_call" | custom-call | tf_op jit(solution)/shard_map/pallas_call | solution.py:314
  289.1 0.0 copy-done.5
  289.1 0.0 copy-start
  289.1 0.0 copy-start.4
  289.2 0.9 copy.32
  290.0 0.8 copy-done
  290.8 0.0 copy-start.3
  290.8 1.1 copy.33
  292.0 0.0 copy-done.4
  292.0 0.0 copy-start.2
  292.0 0.0 copy-start.1
  292.0 0.9 copy.34
  292.9 0.0 copy-done.3
  292.9 0.9 copy.35
  293.8 0.0 copy-done.2
  293.8 0.9 copy.36
  294.7 0.0 copy-done.1
  294.7 0.9 copy.37
  295.6 12.8 %copy.38 = bf16[55328,128]{1,0:T(8,128)(2,1)} copy(bf16[55328,128]{1,0:T(8,128)(2,1)} %shard_map.210) | data formatting | bytes 28327936
  (2 shorter events, 0.0 us)
Async XLA Ops:
  209.8 79.3 %copy-start.5 = (bf16[512,768]{1,0:T(8,128)(2,1)S(1)}, bf16[512,768]{1,0:T(8,128)(2,1)}, u32[]{:S(2)}) copy-start(bf16[512,768]{1,0:T(8,128)(2,1)} %get-tuple-element.58) | copy-start | bytes 2359300
  289.1 1.7 copy-start
  289.1 2.8 copy-start.4
  290.8 2.1 copy-start.3
  292.0 1.8 copy-start.2
  292.0 2.8 copy-start.1

commit v3 on v2

--- a/solution.py
+++ b/solution.py
@@ -88,52 +88,58 @@
 
 
 class Scatter:
-    def __init__(self, grid, first, count, stride, window, base=0, pairs=0):
-        self.g, self.first, self.count, self.stride, self.window = grid, first, count, stride, window
-        self.base, self.pairs = base, pairs
+    def __init__(self, grid, first, planes, stride, window, base, tree):
+        self.g, self.first, self.owners, self.stride, self.window = grid, first, planes, stride, window
+        self.base, self.tree = base, tree
+        self.parts = 2 if window % 32 == 0 else 1
+        self.rows = window // self.parts
+        self.count = planes * self.parts
+        self.levels = grid.planes.bit_length() - 1
+        self.ahead = 3
 
     def scratch(self):
-        g, n, w = self.g, self.count, self.window
+        g, n, w = self.g, self.count, self.rows
         dma = pltpu.SemaphoreType.DMA
+        lines = self.levels * self.owners if self.tree else g.planes - 1
         return [
             pltpu.VMEM((n, g.X, 2, w, 128), bf16),
             pltpu.VMEM((n, g.X, 2, w, 128), bf16),
             pltpu.VMEM((n, g.X - 1, 2, w, 128), bf16),
             pltpu.VMEM((n, w, 128), bf16),
+            pltpu.VMEM((lines, self.parts, w, 128), bf16),
             dma((n, g.X, 2)), dma((n, g.X, 2)), dma((n, g.X, 2)),
             dma((n, g.X - 1, 2)), dma((n, g.X - 1, 2)),
-            dma((n,)), dma((n,)), dma((n,)), dma((g.planes - 1,)),
+            dma((n,)), dma((n,)), dma((n,)), dma((lines, self.parts)),
         ]
 
-    def shared(self):
-        return [
-            pltpu.VMEM((self.g.planes - 1, self.window, 128), bf16),
-            pltpu.VMEM((self.window, 128), bf16),
-        ]
-
-    def bind(self, flat, out, scratch, shared):
-        self.r4, self.kept = shared
-        (self.own, self.r1, self.r2, self.r3, self.lsem, self.s1, self.q1, self.s2,
+    def bind(self, flat, out, scratch):
+        (self.own, self.r1, self.r2, self.r3, self.r4, self.lsem, self.s1, self.q1, self.s2,
          self.q2, self.s3, self.q3, self.s4, self.q4) = scratch
         self.flat, self.out, self.g = flat, out, self.g.here()
 
     def plane_of(self, k):
-        return self.first + lax.rem(self.g.plane + 1 + k, self.count)
+        n, j = self.owners, k // self.parts
+        g = self.g
+        return self.first + lax.rem(g.plane - self.first + n + 1 + j, n)
+
+    def add(self, out, terms):
+        add_rows(out, terms, self.rows, block_of(self.rows))
 
     def copies0(self, k):
         g = self.g
         q = self.plane_of(k)
+        shift = k % self.parts * self.rows - self.base
         for x in range(g.X):
             for y in range(2):
-                there = pl.multiple_of(self.stride * g.index(q, x, 1 - g.core, y) - self.base, 16)
-                here = pl.multiple_of(self.stride * g.index(q, x, g.core, y) - self.base, 16)
+                there = pl.multiple_of(self.stride * g.index(q, x, 1 - g.core, y) + shift, 16)
+                here = pl.multiple_of(self.stride * g.index(q, x, g.core, y) + shift, 16)
                 yield (
                     pltpu.make_async_remote_copy(
-                        self.flat.at[pl.ds(there, self.window), :], self.r1.at[k, x, y],
+                        self.flat.at[pl.ds(there, self.rows), :], self.r1.at[k, x, y],
                         self.s1.at[k, x, y], self.q1.at[k, x, y],
                         device_id=g.device(core=1 - g.core), device_id_type=MESH),
                     pltpu.make_async_copy(
-                        self.flat.at[pl.ds(here, self.window), :], self.own.at[k, x, y], self.lsem.at[k, x, y]),
+                        self.flat.at[pl.ds(here, self.rows), :], self.own.at[k, x, y], self.lsem.at[k, x, y]),
                     x, y)
 
     def copies1(self, k):
@@ -153,18 +159,27 @@
             self.own.at[k, x, y], self.r3.at[k], self.s3.at[k], self.q3.at[k],
             device_id=g.device(b=1 - g.b), device_id_type=MESH)
 
-    def copy3(self, k):
-        g = self.g
-        q = self.plane_of(k)
-        slot = lax.rem(g.plane - q + g.planes, g.planes) - 1
-        slot = jnp.maximum(slot, 0)
+    def distance(self, k):
+        return lax.rem(self.g.plane - self.plane_of(k) + self.g.planes, self.g.planes)
+
+    def copy3(self, k, line, plane):
+        g = self.g
+        part = k % self.parts
         return pltpu.make_async_remote_copy(
-            self.own.at[k, g.x, g.y], self.r4.at[slot], self.s4.at[k], self.q4.at[slot],
-            device_id=g.device(plane=q), device_id_type=MESH)
+            self.own.at[k, g.x, g.y], self.r4.at[line, part], self.s4.at[k], self.q4.at[line, part],
+            device_id=g.device(plane=plane), device_id_type=MESH)
+
+    def climb(self, k, level, wait):
+        far = self.distance(k)
+        line = level * self.owners + self.plane_of(k) - self.first
+
+        @pl.when(lax.rem(far, 2 << level) == 1 << level)
+        def _():
+            copy = self.copy3(k, line, lax.rem(self.g.plane - (1 << level) + self.g.planes, self.g.planes))
+            copy.wait_send() if wait else copy.start()
 
     def step(self, stage, k):
         g = self.g
-        block = block_of(self.window)
         if stage == 0:
             for far, near, x, y in self.copies0(k):
                 far.start()
@@ -173,153 +188,198 @@
             for far, near, x, y in self.copies0(k):
                 near.wait()
                 far.wait()
-                add_rows(self.own.at[k, x, y], [self.own.at[k, x, y], self.r1.at[k, x, y]], self.window, block)
-            for copy in self.copies1(k):
-                copy.start()
+                self.add(self.own.at[k, x, y], [self.own.at[k, x, y], self.r1.at[k, x, y]])
+            if k < self.ahead:
+                for copy in self.copies1(k):
+                    copy.start()
         elif stage == 2:
             for copy in self.copies1(k):
                 copy.wait()
-            for b in range(2):
+            if k + self.ahead < self.count:
+                for copy in self.copies1(k + self.ahead):
+                    copy.start()
+            for b in (1 - g.b, g.b):
                 x, y = g.xy(g.a, b)
                 mine = self.own.at[k, x, y]
-                add_rows(mine, [mine] + [self.r2.at[k, d, b] for d in range(g.X - 1)], self.window, block)
-            self.copy2(k).start()
+                self.add(mine, [mine] + [self.r2.at[k, d, b] for d in range(g.X - 1)])
+                if b is not g.b:
+                    self.copy2(k).start()
         elif stage == 3:
             self.copy2(k).wait()
             mine = self.own.at[k, g.x, g.y]
-            q = self.plane_of(k)
-            add_rows(mine, [mine, self.r3.at[k]], self.window, block)
+            self.add(mine, [mine, self.r3.at[k]])
+            if self.tree:
+                self.climb(k, 0, False)
+            else:
+                far = self.distance(k)
+
+                @pl.when(far > 0)
+                def _():
+                    self.copy3(k, far - 1, self.plane_of(k)).start()
+        else:
+            level = stage - 4
+            far = self.distance(k)
+            mine = self.own.at[k, g.x, g.y]
+            line = level * self.owners + self.plane_of(k) - self.first
+
+            @pl.when(lax.rem(far, 2 << level) == 0)
+            def _():
+                self.copy3(k, line, self.plane_of(k)).wait_recv()
+                self.add(mine, [mine, self.r4.at[line, k % self.parts]])
+
+            if level + 1 < self.levels:
+                self.climb(k, level + 1, False)
+
+    def finish(self):
+        g = self.g
+        for k in range(self.count):
+            if self.tree:
+                for level in range(self.levels):
+                    self.climb(k, level, True)
+            else:
+                @pl.when(self.distance(k) > 0)
+                def _():
+                    self.copy3(k, 0, self.plane_of(k)).wait_send()
+
+    def collect(self):
+        g = self.g
+        for part in range(self.parts):
+            k = (self.owners - 1) * self.parts + part
+            terms = [self.own.at[k, g.x, g.y]]
+            if not self.tree:
+                for d in range(g.planes - 1):
+                    self.copy3(k, d, lax.rem(g.plane + 1 + d, g.planes)).wait_recv()
+                    terms.append(self.r4.at[d, part])
+            self.add(self.out.at[pl.ds(part * self.rows, self.rows), :], terms)
+
+
+class Gather:
+    def __init__(self, grid, stride):
+        self.g, self.stride = grid, stride
+        self.parts = 2 if stride % 32 == 0 else 1
+        self.rows = stride // self.parts
+        self.count = grid.planes * self.parts
+
+    def scratch(self):
+        dma = pltpu.SemaphoreType.DMA
+        n, X, planes, parts = self.count, self.g.X, self.g.planes, self.parts
+        return [dma((parts,)), dma((2 * planes - 1, parts)), dma((planes, parts)), dma((n,)), dma((n,)),
+                dma((n, X - 1, 2)), dma((n, X - 1, 2)), dma((n, X, 2)), dma((n, X, 2))]
+
+    def bind(self, fresh, out, scratch):
+        self.lsem, self.s0, self.q0, self.s1, self.q1, self.s2, self.q2, self.s3, self.q3 = scratch
+        self.fresh, self.out, self.g = fresh, out, self.g.here()
+
+    def plane_of(self, k):
+        g = self.g
+        j = k // self.parts
+        if g.planes == 4:
+            one = jnp.where(g.plane == 0, (0, 1, 2, 3)[j], (1, 2, 0, 3)[j])
+            other = jnp.where(g.plane == 2, (2, 1, 3, 0)[j], (3, 2, 1, 0)[j])
+            return jnp.where(g.plane < 2, one, other)
+        up = g.planes - 1 - g.plane
+        return jnp.where(j <= up, g.plane + j, g.plane - (j - up))
+
+    def part(self, q, x, core, y, part):
+        g = self.g
+        start = self.stride * g.index(q, x, core, y) + part * self.rows
+        return self.out.at[pl.ds(pl.multiple_of(start, 16), self.rows), :]
+
+    def first(self, part):
+        g = self.g
+        return pltpu.make_async_copy(
+            self.fresh.at[pl.ds(part * self.rows, self.rows), :], self.part(g.plane, g.x, g.core, g.y, part), self.lsem.at[part])
+
+    def send0(self, part, way):
+        g = self.g
+        rows = self.part(g.plane, g.x, g.core, g.y, part)
+        slot = way + g.planes - 1
+        return pltpu.make_async_remote_copy(
+            self.fresh.at[pl.ds(part * self.rows, self.rows), :], rows, self.s0.at[slot, part], self.q0.at[g.plane, part],
+            device_id=g.device(plane=jnp.clip(g.plane + way, 0, g.planes - 1)), device_id_type=MESH)
+
+    def came0(self, q, part):
+        g = self.g
+        rows = self.part(q, g.x, g.core, g.y, part)
+        return pltpu.make_async_remote_copy(
+            rows, rows, self.s0.at[0, part], self.q0.at[q, part], device_id=g.device(plane=q), device_id_type=MESH)
+
+    def reach(self, far, wait):
+        g = self.g
+        for part in range(self.parts):
+            for way in (-far, far):
+                @pl.when(jnp.logical_and(g.plane + way >= 0, g.plane + way < g.planes))
+                def _():
+                    copy = self.send0(part, way)
+                    copy.wait_send() if wait else copy.start()
+
+    def send1(self, k):
+        g = self.g
+        rows = self.part(self.plane_of(k), g.x, g.core, g.y, k % self.parts)
+        return pltpu.make_async_remote_copy(
+            rows, rows, self.s1.at[k], self.q1.at[k], device_id=g.device(b=1 - g.b), device_id_type=MESH)
+
+    def send2(self, k):
+        g = self.g
+        for d in range(1, g.X):
+            for b in range(2):
+                x, y = g.xy(g.a, (g.b, 1 - g.b)[b])
+                rows = self.part(self.plane_of(k), x, g.core, y, k % self.parts)
+                yield pltpu.make_async_remote_copy(
+                    rows, rows, self.s2.at[k, d - 1, b], self.q2.at[k, d - 1, b],
+                    device_id=g.device(a=lax.rem(g.a + d, g.X)), device_id_type=MESH)
+
+    def send3(self, k):
+        g = self.g
+        for x in range(g.X):
+            for y in range(2):
+                rows = self.part(self.plane_of(k), x, g.core, y, k % self.parts)
+                yield pltpu.make_async_remote_copy(
+                    rows, rows, self.s3.at[k, x, y], self.q3.at[k, x, y],
+                    device_id=g.device(core=1 - g.core), device_id_type=MESH)
+
+    def begin(self):
+        for far in range(1, self.g.planes):
+            self.reach(far, False)
+        for part in range(self.parts):
+            self.first(part).start()
+
+    def step(self, stage, k):
+        g = self.g
+        q, part = self.plane_of(k), k % self.parts
+        if stage == 0:
+            @pl.when(q == g.plane)
+            def _():
+                self.first(part).wait()
 
             @pl.when(q != g.plane)
             def _():
-                self.copy3(k).start()
-
-            @pl.when(q == g.plane)
-            def _():
-                add_rows(self.kept, [mine], self.window, block)
+                self.came0(q, part).wait_recv()
+
+            self.send1(k).start()
+            for n, copy in enumerate(self.send2(k)):
+                if n % 2 == 0:
+                    copy.start()
+        elif stage == 1:
+            self.send1(k).wait_recv()
+            for n, copy in enumerate(self.send2(k)):
+                if n % 2 == 1:
+                    copy.start()
+        else:
+            for copy in self.send2(k):
+                copy.wait_recv()
+            for copy in self.send3(k):
+                copy.start()
 
     def finish(self):
-        g = self.g
+        for far in range(1, self.g.planes):
+            self.reach(far, True)
         for k in range(self.count):
-            @pl.when(self.plane_of(k) != g.plane)
-            def _():
-                self.copy3(k).wait_send()
-
-        inside = jnp.logical_and(g.plane >= self.first, g.plane < self.first + self.count)
-
-        @pl.when(inside)
-        def _():
-            for d in range(g.planes - 1):
-                pltpu.make_async_remote_copy(
-                    self.kept, self.r4.at[d], self.s4.at[0], self.q4.at[d],
-                    device_id=g.device(plane=lax.rem(g.plane + 1 + d, g.planes)), device_id_type=MESH).wait_recv()
-            add_rows(self.out, [self.kept] + [self.r4.at[d] for d in range(g.planes - 1)], self.window,
-                     block_of(self.window))
-
-    def order(self):
-        found = [(1, k) for k in range(self.count)]
-        for t in range(self.count + 1):
-            found += [(stage, k) for stage, k in ((2, t), (3, t - 1)) if 0 <= k < self.count]
-        return found
-
-    def all(self):
-        for k in range(self.count):
-            self.step(0, k)
-        for stage, k in self.order():
-            self.step(stage, k)
-        self.finish()
-
-
-def gather_kernel(grid, stride, fresh, tail, out, lsem, tsem, s0, q0, s1, q1, s2, q2, s3, q3):
-    g = grid.here()
-    enter(g.partners())
-    X, planes = g.X, g.planes
-
-    def rows(q, x, core, y):
-        return out.at[pl.ds(pl.multiple_of(stride * g.index(q, x, core, y), 16), stride), :]
-
-    mine = rows(g.plane, g.x, g.core, g.y)
-    first = pltpu.make_async_copy(fresh, mine, lsem)
-    first.start()
-    rest = pltpu.make_async_copy(tail, out.at[pl.ds(stride * g.devices, g.devices), :], tsem)
-    rest.start()
-
-    def send0(d):
-        return pltpu.make_async_remote_copy(
-            fresh, mine, s0.at[d - 1], q0.at[d - 1],
-            device_id=g.device(plane=lax.rem(g.plane + d, planes)), device_id_type=MESH)
-
-    def plane_of(k):
-        return lax.rem(g.plane - k + planes, planes)
-
-    def send1(k):
-        part = rows(plane_of(k), g.x, g.core, g.y)
-        return pltpu.make_async_remote_copy(
-            part, part, s1.at[k], q1.at[k], device_id=g.device(b=1 - g.b), device_id_type=MESH)
-
-    def send2(k):
-        for d in range(1, X):
-            for b in range(2):
-                x, y = g.xy(g.a, b)
-                part = rows(plane_of(k), x, g.core, y)
-                yield pltpu.make_async_remote_copy(
-                    part, part, s2.at[k, d - 1, b], q2.at[k, d - 1, b],
-                    device_id=g.device(a=lax.rem(g.a + d, X)), device_id_type=MESH)
-
-    def send3(k):
-        for x in range(X):
-            for y in range(2):
-                part = rows(plane_of(k), x, g.core, y)
-                yield pltpu.make_async_remote_copy(
-                    part, part, s3.at[k, x, y], q3.at[k, x, y],
-                    device_id=g.device(core=1 - g.core), device_id_type=MESH)
-
-    for d in range(1, planes):
-        send0(d).start()
-    first.wait()
-    for t in range(planes + 2):
-        if t < planes:
-            if t > 0:
-                send0(t).wait_recv()
-            send1(t).start()
-        k = t - 1
-        if 0 <= k < planes:
-            send1(k).wait_recv()
-            for copy in send2(k):
-                copy.start()
-        k = t - 2
-        if 0 <= k < planes:
-            for copy in send2(k):
-                copy.wait_recv()
-            for copy in send3(k):
-                copy.start()
-    for k in range(planes):
-        for copy in send3(k):
-            copy.wait_recv()
-    for d in range(1, planes):
-        send0(d).wait_send()
-    for k in range(planes):
-        send1(k).wait_send()
-        for copy in send2(k):
-            copy.wait_send()
-        for copy in send3(k):
-            copy.wait_send()
-    rest.wait()
-
-
-def gather_rows(fresh, tail, grid, stride, collective_id):
-    dma = pltpu.SemaphoreType.DMA
-    n, X = grid.planes, grid.X
-    total = (stride + 1) * grid.devices
-    return pl.pallas_call(
-        functools.partial(gather_kernel, grid, stride),
-        out_shape=jax.ShapeDtypeStruct((total, 128), bf16),
-        in_specs=[pl.BlockSpec(memory_space=pl.ANY)] * 2,
-        out_specs=pl.BlockSpec(memory_space=pl.ANY),
-        scratch_shapes=[dma, dma, dma((n - 1,)), dma((n - 1,)), dma((n,)), dma((n,)),
-                        dma((n, X - 1, 2)), dma((n, X - 1, 2)), dma((n, X, 2)), dma((n, X, 2))],
-        compiler_params=pltpu.CompilerParams(collective_id=collective_id, has_side_effects=True),
-    )(fresh, tail)
+            self.send1(k).wait_send()
+            for copy in self.send2(k):
+                copy.wait_send()
+            for copy in self.send3(k):
+                copy.wait()
 
 
 def lane_mask(rows, head):
@@ -362,12 +422,26 @@
 
 def ffn_kernel(steps, tall, bases, length, x_ref, mixed_ref, cot_ref, gain_ref, wo_ref, wg_ref, wu_ref, wd_ref,
                out_ref, ghid_ref, gmix_ref, ggain_ref, flat_ref,
-               flat, wide, hidden, nf, nft, gout, gate_low, up_low, out_sum, gnf_sum, sems):
+               flat, wide, hidden, nf, nft, gout, gate_low, up_low, out_sum, gnf_sum, sems, lo_send, lo_in, turn):
     step = pl.program_id(0)
     rows, width = x_ref.shape
     chunk = wg_ref.shape[1]
     o_base, g_base, u_base, d_base, end = bases
-    parts = wg_ref.shape[0] // 128
+    dp, y = lax.axis_index("dp"), lax.axis_index("group")
+    core = lax.rem(dp, 2)
+    twin = (dp - core + y, core)
+    moved = core != y
+    lo_copy = lambda: pltpu.make_async_remote_copy(
+        lo_send, lo_in, turn.at[0], turn.at[1], device_id=twin, device_id_type=MESH)
+
+    @pl.when(jnp.logical_and(step == 0, moved))
+    def _():
+        barrier = pltpu.get_barrier_semaphore()
+        pl.semaphore_signal(barrier, inc=1, device_id=twin, device_id_type=MESH)
+
+    @pl.when(jnp.logical_and(step == steps - 1, moved))
+    def _():
+        pl.semaphore_wait(pltpu.get_barrier_semaphore(), 1)
 
     @pl.when(step == 0)
     def _():
@@ -408,7 +482,14 @@
 
     @pl.when(step == steps - 1)
     def _():
-        out_ref[...] = out_sum[...].astype(bf16)
+        low = out_sum[...].astype(bf16)
+        out_ref[...] = low
+
+        @pl.when(moved)
+        def _():
+            lo_send[...] = low
+            lo_copy().start()
+
         total = hidden[...]
         scale = lax.rsqrt(jnp.mean(total * total, axis=1, keepdims=True) + 1e-06)
         unit = total * scale
@@ -454,8 +535,13 @@
                 pltpu.make_async_copy(flat.at[part, :], flat_ref.at[part, :], sems.at[steps + k * turns + turn + 1]).wait()
         last.wait()
 
-
-def ffn(length, x, mixed, cot, gain, wo, wg, wu, wd, pad_rows):
+        @pl.when(moved)
+        def _():
+            lo_copy().wait()
+            out_ref[...] = lo_in[...]
+
+
+def ffn(length, x, mixed, cot, gain, wo, wg, wu, wd, pad_rows, collective_id):
     rows, width = x.shape
     deep = wg.shape[1]
     chunk, tall = 256, 256
@@ -484,8 +570,9 @@
             pltpu.VMEM((rows, width), f32), pltpu.VMEM((rows, width), bf16), pltpu.VMEM((width, rows), bf16),
             pltpu.VMEM((rows, width), bf16), pltpu.VMEM((rows, deep), bf16), pltpu.VMEM((rows, deep), bf16),
             pltpu.VMEM((rows, width), f32), pltpu.VMEM((rows, width), f32),
-            pltpu.SemaphoreType.DMA((steps + 2 * turns + 2,))],
-        compiler_params=pltpu.CompilerParams(vmem_limit_bytes=56 << 20),
+            pltpu.SemaphoreType.DMA((steps + 2 * turns + 2,)),
+            pltpu.VMEM((rows, width), bf16), pltpu.VMEM((rows, width), bf16), pltpu.SemaphoreType.DMA((2,))],
+        compiler_params=pltpu.CompilerParams(collective_id=collective_id, has_side_effects=True, vmem_limit_bytes=56 << 20),
     )(length, x, mixed, cot, gain, wo, wg, wu, wd)
 
 
@@ -724,18 +811,17 @@
     return found
 
 
-def back_kernel(grid, chunk, early, late, ends, heads, buckets, *refs):
+def back_kernel(grid, chunk, early, late, ends, spread, heads, buckets, *refs):
     (q_ref, k_ref, v_ref, gm_ref, mixed_ref, prob_ref, normed_ref, x_ref, ghid_ref, gain_ref, wq_ref, wk_ref, wv_ref,
-     lo_ref, ggain_ref, m1_ref, m2_ref, ma_ref, flat_ref,
-     lo_out, gtok_out, gshard_out, m1_out, m2_out, ma_out, fresh_out, ftail_out) = refs[:27]
-    rest = refs[27:]
+     ggain_ref, m1_ref, m2_ref, ma_ref, flat_ref,
+     gtok_out, gshard_out, m1_out, m2_out, ma_out, copy_out) = refs[:24]
+    rest = refs[24:]
     taken = []
-    for job in (early, late, ends):
+    for job in (early, late, ends, spread):
         size = len(job.scratch())
         taken.append(rest[:size])
         rest = rest[size:]
-    shared, rest = rest[:2], rest[2:]
-    (slope, gq, gk, gv, rk, rv, flat, wide, diag, far, lo_in, gt_in, halo, halo_in, summed, renewed,
+    (slope, gq, gk, gv, rk, rv, flat, wide, diag, far, gt_in, halo, halo_in, summed, renewed, fresh, ftail,
      lsem, s_kv, r_kv, s_turn, r_turn) = rest
     g = grid.here()
     step = pl.program_id(0)
@@ -757,26 +843,30 @@
     prior = (lax.div(before, 2), lax.rem(before, 2))
     shard = ma_ref.shape[0]
     stride, window = early.stride, early.window
-    early.bind(flat_ref, summed.at[pl.ds(count, window), :], taken[0], shared)
-    late.bind(flat, summed.at[pl.ds(count, window), :], taken[1], shared)
+    early.bind(flat_ref, summed.at[pl.ds(count, window), :], taken[0])
+    late.bind(flat, summed.at[pl.ds(count, window), :], taken[1])
     ends.bind(taken[2])
-    order = early.order()
+    spread.bind(fresh, copy_out, taken[3])
+    owner = g.plane >= early.first
+    agenda = [(early, 1, k) for k in range(early.count)]
+    split = early.count - 1
+    jobs = [(early, k) for k in range(early.count)]
+    jobs[split:split] = [(late, k) for k in range(late.count)]
+    for n in range(len(jobs) + 1):
+        agenda += [(job, stage, k) for stage, m in ((2, n), (3, n - 1)) if 0 <= m < len(jobs) for job, k in (jobs[m],)]
     square = width * width // 128
     over = flat.shape[0] - 3 * square
     edge = lambda: pltpu.make_async_copy(flat_ref.at[pl.ds(0, over), :], flat.at[pl.ds(3 * square, over), :], lsem.at[0])
-    lo_copy = lambda: pltpu.make_async_remote_copy(
-        lo_ref, lo_in, s_turn.at[0], r_turn.at[0], device_id=twin, device_id_type=MESH)
     ghid_copy = lambda: pltpu.make_async_copy(ghid_ref, gtok_out, lsem.at[1])
-    lo_stay = lambda: pltpu.make_async_copy(lo_ref, lo_in, r_turn.at[0])
     gt_copy = lambda: pltpu.make_async_remote_copy(
-        gq, gt_in, s_turn.at[1], r_turn.at[1], device_id=twin, device_id_type=MESH)
+        gq, gt_in, s_turn.at[0], r_turn.at[0], device_id=twin, device_id_type=MESH)
     halo_copy = lambda: pltpu.make_async_remote_copy(
-        halo, halo_in, s_turn.at[2], r_turn.at[2], device_id=nextdoor, device_id_type=MESH)
+        halo, halo_in, s_turn.at[1], r_turn.at[1], device_id=nextdoor, device_id_type=MESH)
 
     def square_grad(right, base):
-        half = width // 2
-        for k in range(2):
-            flatten_into(dot_of(normed_ref[:, half * k : half * k + half], right, TN), wide, flat, base + k * square // 2)
+        third = width // 3
+        for k in range(3):
+            flatten_into(dot_of(normed_ref[:, third * k : third * k + third], right, TN), wide, flat, base + k * square // 3)
 
     @pl.when(step == 0)
     def _():
@@ -798,19 +888,21 @@
             halo[k] = state[pl.ds(shard - count, count), :]
         halo_copy().start()
 
-        @pl.when(moved)
-        def _():
-            lo_copy().start()
-
-        @pl.when(jnp.logical_not(moved))
-        def _():
-            lo_stay().start()
-
-    for n, (stage, k) in enumerate(order):
-        if n + 1 < late.pairs:
-            @pl.when(step == n + 1)
-            def _():
-                early.step(stage, k)
+    shares = [early.count * 2 // 6, early.count * 4 // 6, early.count * 5 // 6, early.count, early.count + 1]
+    for n, (start, stop) in enumerate(zip([0] + shares[:-1], shares)):
+        @pl.when(step == n + 1)
+        def _():
+            for job, stage, k in agenda[start:stop]:
+                job.step(stage, k)
+
+    pending = agenda[shares[-1] :]
+    pending += [(late, 4 + level, k) for level in range(late.levels) for k in range(late.count)]
+
+    def due(count, late_too=False):
+        for _ in range(count):
+            if pending and (late_too or pending[0][0] is early):
+                job, stage, k = pending.pop(0)
+                job.step(stage, k)
 
     @pl.when(step < pairs)
     def _():
@@ -863,15 +955,18 @@
             copy.start()
         square_grad(gq[...], 0)
         total = dot_of(gq[...], wq_ref[...], NT)
+        due(1)
         for k, (a, b, w) in enumerate(((gk, rk, wk_ref), (gv, rv, wv_ref))):
             copies[k].wait()
             low = (a[mine, :].astype(f32) + b[...].astype(f32)).astype(bf16)
             b[...] = low
             square_grad(low, (k + 1) * square)
             total = total + dot_of(low, w[...], NT)
+            due(2)
         edge().wait()
         for k in range(late.count):
             late.step(0, k)
+        due(2)
         x = x_ref[...].astype(f32)
         scale = lax.rsqrt(jnp.mean(x * x, axis=1, keepdims=True) + 1e-06)
         unit = x * scale
@@ -885,6 +980,10 @@
         def _():
             gq[...] = gtok.astype(bf16)
             gt_copy().start()
+
+        for k in range(late.count):
+            late.step(1, k)
+        due(2, True)
 
         tail = ends.mine(0)
         tail[...] = jnp.zeros(tail.shape, f32)
@@ -896,58 +995,76 @@
         for k in range(3):
             tail[16 + k * count : 16 + (k + 1) * count, :] = jnp.where(place == count - 1, halo[k], 0.0)
         ends.start(0)
-
-        left = [(early, stage, k) for n, (stage, k) in enumerate(order) if n + 1 >= late.pairs]
-        left += [(late, stage, k) for stage, k in late.order()]
-        for n, (job, stage, k) in enumerate(left):
-            job.step(stage, k)
-            if n < 3:
-                found = ends.done(n)
-                ends.mine(n + 1)[...] = found
-                ends.start(n + 1)
+        for n in range(3):
+            due(1, True)
+            found = ends.done(n)
+            ends.mine(n + 1)[...] = found
+            ends.start(n + 1)
+        due(len(pending), True)
         found = ends.done(3)
+        grads = jnp.concatenate([found[:16], jnp.zeros((count - 16, 128), f32)], axis=0)
+        last = [found[16 + k * count : 16 + (k + 1) * count] for k in range(3)]
+        ftail[...] = adam_step(grads, *last)[2].astype(bf16)
+        rest_copy = pltpu.make_async_copy(ftail, copy_out.at[pl.ds(stride * count, count), :], lsem.at[0])
+        rest_copy.start()
+        halo_copy().wait()
         summed[pl.ds(0, count), :] = jnp.zeros((count, 128), f32)
+
+        def renew(job):
+            job.collect()
+
+            @pl.when(place == count - 1)
+            def _():
+                summed[pl.ds(count + stride, count), :] = grads
+
+            renewed[pl.ds(0, count), :] = adam_step(summed[pl.ds(place, count), :], *[halo_in[k] for k in range(3)])[2]
+            for start in range(0, shard, 216):
+                size = min(216, shard - start)
+                part = pl.ds(start, size)
+                own = summed[pl.ds(place + count + start, size), :]
+                one, two, new = adam_step(own, m1_ref[part, :], m2_ref[part, :], ma_ref[part, :])
+                gshard_out[part, :] = own
+                m1_out[part, :] = one
+                m2_out[part, :] = two
+                ma_out[part, :] = new
+                renewed[pl.ds(count + start, size), :] = new
+            for start in range(0, stride, stride // 8):
+                fresh[pl.ds(start, stride // 8), :] = renewed[pl.ds(start + count - place, stride // 8), :].astype(bf16)
+
+        own = range(spread.parts)
+
+        def open_own():
+            spread.begin()
+            for k in own:
+                spread.step(0, k)
+
+        @pl.when(owner)
+        def _():
+            renew(early)
+
+        @pl.when(jnp.logical_not(owner))
+        def _():
+            renew(late)
+
+        open_own()
+        for n in range(spread.count + 2):
+            for stage in (0, 1, 2):
+                k = n - stage
+                if 0 <= k < spread.count and (stage, k) not in [(0, k) for k in own]:
+                    spread.step(stage, k)
         early.finish()
         late.finish()
-
-        @pl.when(place == count - 1)
-        def _():
-            summed[pl.ds(count + stride, count), :] = jnp.zeros((count, 128), f32)
-            summed[pl.ds(count + stride, 16), :] = found[:16]
-
-        grads = jnp.concatenate([found[:16], jnp.zeros((count - 16, 128), f32)], axis=0)
-        last = [found[16 + k * count : 16 + (k + 1) * count] for k in range(3)]
-        ftail_out[...] = adam_step(grads, *last)[2].astype(bf16)
-        halo_copy().wait()
-        renewed[pl.ds(0, count), :] = adam_step(summed[pl.ds(place, count), :], *[halo_in[k] for k in range(3)])[2]
-        for start in range(0, shard, 216):
-            size = min(216, shard - start)
-            part = pl.ds(start, size)
-            grads = summed[pl.ds(place + count + start, size), :]
-            one, two, new = adam_step(grads, m1_ref[part, :], m2_ref[part, :], ma_ref[part, :])
-            gshard_out[part, :] = grads
-            m1_out[part, :] = one
-            m2_out[part, :] = two
-            ma_out[part, :] = new
-            renewed[pl.ds(count + start, size), :] = new
-        for start in range(0, stride, stride // 8):
-            fresh_out[pl.ds(start, stride // 8), :] = renewed[pl.ds(start + count - place, stride // 8), :].astype(bf16)
+        spread.finish()
+        rest_copy.wait()
 
         @pl.when(moved)
         def _():
-            lo_copy().wait()
             gt_copy().wait()
             gtok_out[...] = gt_in[...].astype(f32)
 
-        @pl.when(jnp.logical_not(moved))
-        def _():
-            lo_stay().wait()
-
-        lo_out[...] = lo_in[...]
-
 
 def back(grid, heads, buckets, query, keys_all, values_all, grad_mixed, mixed, prob, normed, x, grad_hidden, gain,
-         wq, wk, wv, layer_out, ggain, moment_one, moment_two, master, flat, collective_id):
+         wq, wk, wv, ggain, moment_one, moment_two, master, flat, collective_id):
     rows, width = query.shape
     span = keys_all.shape[0]
     pairs = width // 128
@@ -956,39 +1073,41 @@
     stride, window = shard - 1, shard - 1 + count
     cut = grid.planes // 4
     late_rows = 3 * width * width // 128
-    early = Scatter(grid, cut, grid.planes - cut, stride, window, late_rows, pairs)
-    late = Scatter(grid, 0, cut, stride, window, 0, pairs)
+    early = Scatter(grid, cut, grid.planes - cut, stride, window, late_rows, False)
+    late = Scatter(grid, 0, cut, stride, window, 0, True)
+    spread = Gather(grid, stride)
     ends = TailSum(grid, 16 + 3 * count)
     at = lambda s: jnp.minimum(s, pairs - 1)
     tall = lambda n: pl.BlockSpec((n, 128), lambda s: (0, at(s)))
     dma = pltpu.SemaphoreType.DMA
     state = (shard, 128)
     return pl.pallas_call(
-        functools.partial(back_kernel, grid, 256, early, late, ends, heads, buckets),
+        functools.partial(back_kernel, grid, 256, early, late, ends, spread, heads, buckets),
         grid=(pairs + 1,),
         in_specs=[tall(rows), tall(span), tall(span), tall(rows), tall(rows),
                   pl.BlockSpec((2, span, rows), lambda s: (at(s), 0, 0)),
                   once((rows, width)), once((rows, width)), pl.BlockSpec(memory_space=pl.ANY), once((1, width)),
                   once((width, width)), once((width, width)), once((width, width)),
-                  pl.BlockSpec(memory_space=pl.ANY), once((1, width)), once(state), once(state), once(state),
+                  once((1, width)), once(state), once(state), once(state),
                   pl.BlockSpec(memory_space=pl.ANY)],
-        out_specs=[once((rows, width)), once((rows, width)), once(state), once(state), once(state), once(state),
-                   once((stride, 128)), once((count, 128))],
+        out_specs=[once((rows, width)), once(state), once(state), once(state), once(state),
+                   pl.BlockSpec(memory_space=pl.ANY)],
         out_shape=[jax.ShapeDtypeStruct(s, t) for s, t in (
-            ((rows, width), bf16), ((rows, width), f32), (state, f32), (state, f32), (state, f32), (state, f32),
-            ((stride, 128), bf16), ((count, 128), bf16))],
-        scratch_shapes=early.scratch() + late.scratch() + ends.scratch() + early.shared() + [
+            ((rows, width), f32), (state, f32), (state, f32), (state, f32), (state, f32),
+            (((stride + 1) * count, 128), bf16))],
+        scratch_shapes=early.scratch() + late.scratch() + ends.scratch() + spread.scratch() + [
             pltpu.VMEM((2, span, rows), bf16), pltpu.VMEM((rows, width), bf16),
             pltpu.VMEM((span, width), bf16), pltpu.VMEM((span, width), bf16),
             pltpu.VMEM((rows, width), bf16), pltpu.VMEM((rows, width), bf16),
-            pltpu.VMEM((late_rows + count, 128), bf16), pltpu.VMEM((late_rows // 6, 128), f32),
+            pltpu.VMEM((late_rows + count, 128), bf16), pltpu.VMEM((late_rows // 9, 128), f32),
             pltpu.VMEM((3, 16, 256), f32), pltpu.VMEM((2, 16, 128), f32),
-            pltpu.VMEM((rows, width), bf16), pltpu.VMEM((rows, width), bf16),
+            pltpu.VMEM((rows, width), bf16),
             pltpu.VMEM((3, count, 128), f32), pltpu.VMEM((3, count, 128), f32),
             pltpu.VMEM((count + window, 128), f32), pltpu.VMEM((count + shard + 7, 128), f32),
-            dma((2,)), dma((2,)), dma((2,)), dma((3,)), dma((3,))],
+            pltpu.VMEM((stride, 128), bf16), pltpu.VMEM((count, 128), bf16),
+            dma((2,)), dma((2,)), dma((2,)), dma((2,)), dma((2,))],
         compiler_params=pltpu.CompilerParams(collective_id=collective_id, has_side_effects=True, vmem_limit_bytes=62 << 20),
-    )(query, keys_all, values_all, grad_mixed, mixed, prob, normed, x, grad_hidden, gain, wq, wk, wv, layer_out, ggain,
+    )(query, keys_all, values_all, grad_mixed, mixed, prob, normed, x, grad_hidden, gain, wq, wk, wv, ggain,
       moment_one, moment_two, master, flat)
 
 
@@ -1005,11 +1124,10 @@
     x, cot, lens, normed, query, keys_all, values_all, mixed, prob = front(
         grid, tokens, cotangent, lens, gain_one, w_query, w_keys, w_values, near, 1)
     layer_out, grad_hidden, grad_mixed, grad_gain_ffn, flat = ffn(
-        lens, x, mixed, cot, gain_two, w_output, w_gate, w_up, w_down, count)
-    layer_out, grad_tokens, grad_shard, moment_one_new, moment_two_new, master_new, fresh, fresh_tail = back(
+        lens, x, mixed, cot, gain_two, w_output, w_gate, w_up, w_down, count, 3)
+    grad_tokens, grad_shard, moment_one_new, moment_two_new, master_new, fresh_copy = back(
         grid, bias_table.shape[1], bias_table.shape[0], query, keys_all, values_all, grad_mixed, mixed, prob, normed, x,
-        grad_hidden, gain_one, w_query, w_keys, w_values, layer_out, grad_gain_ffn, moment_one, moment_two, master, flat, 2)
-    fresh_copy = gather_rows(fresh, fresh_tail, grid, master.shape[0] - 1, 3)
+        grad_hidden, gain_one, w_query, w_keys, w_values, grad_gain_ffn, moment_one, moment_two, master, flat, 2)
     return (layer_out, grad_tokens, grad_shard, moment_one_new, moment_two_new, master_new, fresh_copy)
 
 

time: 312 us -> 270 us (0.87)
  Pallas kernels: 283 us -> 243 us
    pallas_call x1 -> x0, Pallas kernels: 79.3 us -> none  [gather_rows(): pl.pallas_call(functools.partial(gather_kernel, grid, stride), out_shape=...]
    pallas_call x1, Pallas kernels: 134 us -> 174 us  [back(): pl.pallas_call(functools.partial(back_kernel, grid, 256, early, late, end...]
where the time goes in v3:
time: 270 us; the launch traced here: 269 us
  Pallas kernels  243 us (90%)
  local copies, waits for them, and re-layouts  22.4 us (8%)
    pallas_call x1, Pallas kernels, back(): pl.pallas_call(functools.partial(back_kernel, grid, 256, early, late, end...  174 us
    pallas_call x1, Pallas kernels, front(): pl.pallas_call(functools.partial(front_kernel, grid, 256), grid=(pairs,),...  40 us
    pallas_call x1, Pallas kernels, ffn(): pl.pallas_call(functools.partial(ffn_kernel, steps, tall, bases), grid=(s...  29.7 us
    unnamed x19, local copies, waits for them, and re-layouts  19.3 us

profile of v3, /device:TPU:0, one launch (start us, length us, event | category | flops | bytes accessed | tf_op | source)
XLA Modules:
  0.0 269.0 jit_solution(10219321900541569663)
XLA Ops:
  1.3 1.3 reshape.83.gain_ref.refs_9_
  2.6 1.3 reshape.84.gain_ref
  3.8 0.6 broadcast_in_dim.34.len_ref
  4.4 0.1 fusion
  4.5 0.7 convert_element_type.68
  5.2 1.1 select_reduce_fusion.y_ref
  6.3 40.0 %shard_map.207 = (bf16[512,768]{1,0:T(8,128)(2,1)}, bf16[512,768]{1,0:T(8,128)(2,1)}, s32[8,128]{1,0:T(8,128)}, bf16[512,768]{1,0:T(8,128)(2,1)}, bf16[512,768]{...) custom-call(bf16[512,768]{1,0:T(8,128)(2,1)} %tok_ref.1, ...), custom_call_target="tpu_custom_call" | custom-call | tf_op jit(solution)/shard_map/pallas_call | solution.py:700
  46.3 29.7 %shard_map.208 = (bf16[512,768]{1,0:T(8,128)(2,1)}, f32[512,768]{1,0:T(8,128)}, bf16[512,768]{1,0:T(8,128)(2,1)}, f32[1,768]{1,0:T(1,128)}, bf16[41504,128]{1,0:T(8,128)(2,1)}) custom-call(s32[8,128]{1,0:T(8,128)} %get-tuple-element.27.length, bf16[512,768]{1,0:T(8,128)(2,1)} %get-tuple-element.28.x_ref.refs_7_, ...), custom_call_target="tpu_custom_call" | custom-call | tf_op jit(solution)/shard_map/pallas_call | solution.py:555
  76.0 0.0 copy-start.5
  76.0 173.7 %shard_map.209 = (f32[512,768]{1,0:T(8,128)}, f32[1729,128]{1,0:T(8,128)}, f32[1729,128]{1,0:T(8,128)}, f32[1729,128]{1,0:T(8,128)}, f32[1729,128]{1,0:T(8,128)}, /*index=5*/bf16[55328,128]{1,0:T(8,128)(2,1)}) custom-call(bf16[512,768]{1,0:T(8,128)(2,1)} %get-tuple-element.32.refs_0_, bf16[1024,768]{1,0:T(8,128)(2,1)} %get-tuple-element.33.refs_1_, ...), custom_call_target="tpu_custom_call" | custom-call | tf_op jit(solution)/shard_map/pallas_call | solution.py:1084
  249.7 0.0 copy-start
  249.7 0.0 copy-done.5
  249.7 0.0 copy-start.4
  249.8 0.9 copy.32
  250.6 0.8 copy-done
  251.4 0.0 copy-start.3
  251.4 1.1 copy.33
  252.6 0.0 copy-done.4
  252.6 0.0 copy-start.2
  252.6 0.0 copy-start.1
  252.6 0.9 copy.34
  253.5 0.0 copy-done.3
  253.5 0.9 copy.35
  254.4 0.0 copy-done.2
  254.4 0.9 copy.36
  255.3 0.0 copy-done.1
  255.3 0.9 copy.37
  256.2 12.8 %copy.38 = bf16[55328,128]{1,0:T(8,128)(2,1)} copy(bf16[55328,128]{1,0:T(8,128)(2,1)} %get-tuple-element.60) | data formatting | bytes 28327936
  (2 shorter events, 0.0 us)
Async XLA Ops:
  76.0 173.7 %copy-start.5 = (bf16[512,768]{1,0:T(8,128)(2,1)S(1)}, bf16[512,768]{1,0:T(8,128)(2,1)}, u32[]{:S(2)}) copy-start(bf16[512,768]{1,0:T(8,128)(2,1)} %get-tuple-element.54) | copy-start | bytes 2359300
  249.7 1.7 copy-start
  249.7 2.8 %copy-start.4 = (f32[1729,128]{1,0:T(8,128)S(1)}, f32[1729,128]{1,0:T(8,128)}, u32[]{:S(2)}) copy-start(f32[1729,128]{1,0:T(8,128)} %get-tuple-element.56) | copy-start | bytes 2655748
  251.4 2.1 copy-start.3
  252.6 1.8 copy-start.2
  252.6 2.8 %copy-start.1 = (f32[1729,128]{1,0:T(8,128)S(1)}, f32[1729,128]{1,0:T(8,128)}, u32[]{:S(2)}) copy-start(f32[1729,128]{1,0:T(8,128)} %get-tuple-element.59) | copy-start | bytes 2655748

commit v4 on v3

--- a/solution.py
+++ b/solution.py
@@ -95,7 +95,7 @@
         self.rows = window // self.parts
         self.count = planes * self.parts
         self.levels = grid.planes.bit_length() - 1
-        self.ahead = 3
+        self.ahead = 6
 
     def scratch(self):
         g, n, w = self.g, self.count, self.rows
@@ -256,7 +256,7 @@
 class Gather:
     def __init__(self, grid, stride):
         self.g, self.stride = grid, stride
-        self.parts = 2 if stride % 32 == 0 else 1
+        self.parts = 3 if stride % 48 == 0 else 1
         self.rows = stride // self.parts
         self.count = grid.planes * self.parts
 

time: 270 us -> 268 us (level)
  no operation moved by 1% of the time
where the time goes in v4:
time: 268 us
  Pallas kernels  242 us (90%)
  local copies, waits for them, and re-layouts  22.4 us (8%)
    pallas_call x1, Pallas kernels, back(): pl.pallas_call(functools.partial(back_kernel, grid, 256, early, late, end...  173 us
    pallas_call x1, Pallas kernels, front(): pl.pallas_call(functools.partial(front_kernel, grid, 256), grid=(pairs,),...  40 us
    pallas_call x1, Pallas kernels, ffn(): pl.pallas_call(functools.partial(ffn_kernel, steps, tall, bases), grid=(s...  29.7 us
    unnamed x19, local copies, waits for them, and re-layouts  19.3 us

profile of v4, /device:TPU:0, one launch (start us, length us, event | category | flops | bytes accessed | tf_op | source)
XLA Modules:
  0.0 267.9 jit_solution(8900519566335960612)
XLA Ops:
  1.3 1.3 reshape.83.gain_ref.refs_9_
  2.6 1.3 reshape.84.gain_ref
  3.8 0.6 broadcast_in_dim.34.len_ref
  4.4 0.1 fusion
  4.5 0.7 convert_element_type.68
  5.2 1.1 select_reduce_fusion.y_ref
  6.3 40.0 %shard_map.207 = (bf16[512,768]{1,0:T(8,128)(2,1)}, bf16[512,768]{1,0:T(8,128)(2,1)}, s32[8,128]{1,0:T(8,128)}, bf16[512,768]{1,0:T(8,128)(2,1)}, bf16[512,768]{...) custom-call(bf16[512,768]{1,0:T(8,128)(2,1)} %tok_ref.1, ...), custom_call_target="tpu_custom_call" | custom-call | tf_op jit(solution)/shard_map/pallas_call | solution.py:700
  46.3 29.7 %shard_map.208 = (bf16[512,768]{1,0:T(8,128)(2,1)}, f32[512,768]{1,0:T(8,128)}, bf16[512,768]{1,0:T(8,128)(2,1)}, f32[1,768]{1,0:T(1,128)}, bf16[41504,128]{1,0:T(8,128)(2,1)}) custom-call(s32[8,128]{1,0:T(8,128)} %get-tuple-element.27.length, bf16[512,768]{1,0:T(8,128)(2,1)} %get-tuple-element.28.x_ref.refs_7_, ...), custom_call_target="tpu_custom_call" | custom-call | tf_op jit(solution)/shard_map/pallas_call | solution.py:555
  76.0 0.0 copy-start.5
  76.0 172.6 %shard_map.209 = (f32[512,768]{1,0:T(8,128)}, f32[1729,128]{1,0:T(8,128)}, f32[1729,128]{1,0:T(8,128)}, f32[1729,128]{1,0:T(8,128)}, f32[1729,128]{1,0:T(8,128)}, /*index=5*/bf16[55328,128]{1,0:T(8,128)(2,1)}) custom-call(bf16[512,768]{1,0:T(8,128)(2,1)} %get-tuple-element.32.refs_0_, bf16[1024,768]{1,0:T(8,128)(2,1)} %get-tuple-element.33.refs_1_, ...), custom_call_target="tpu_custom_call" | custom-call | tf_op jit(solution)/shard_map/pallas_call | solution.py:1084
  248.6 0.0 copy-start
  248.6 0.0 copy-done.5
  248.6 0.0 copy-start.4
  248.6 0.9 copy.32
  249.5 0.8 copy-done
  250.3 0.0 copy-start.3
  250.3 1.1 copy.33
  251.4 0.0 copy-done.4
  251.5 0.0 copy-start.2
  251.5 0.0 copy-start.1
  251.5 0.9 copy.34
  252.4 0.0 copy-done.3
  252.4 0.9 copy.35
  253.3 0.0 copy-done.2
  253.3 0.9 copy.36
  254.2 0.0 copy-done.1
  254.2 0.9 copy.37
  255.1 12.8 %copy.38 = bf16[55328,128]{1,0:T(8,128)(2,1)} copy(bf16[55328,128]{1,0:T(8,128)(2,1)} %get-tuple-element.60) | data formatting | bytes 28327936
  (2 shorter events, 0.0 us)
Async XLA Ops:
  76.0 172.6 %copy-start.5 = (bf16[512,768]{1,0:T(8,128)(2,1)S(1)}, bf16[512,768]{1,0:T(8,128)(2,1)}, u32[]{:S(2)}) copy-start(bf16[512,768]{1,0:T(8,128)(2,1)} %get-tuple-element.54) | copy-start | bytes 2359300
  248.6 1.7 copy-start
  248.6 2.8 %copy-start.4 = (f32[1729,128]{1,0:T(8,128)S(1)}, f32[1729,128]{1,0:T(8,128)}, u32[]{:S(2)}) copy-start(f32[1729,128]{1,0:T(8,128)} %get-tuple-element.56) | copy-start | bytes 2655748
  250.3 2.1 copy-start.3
  251.5 1.8 copy-start.2
  251.5 2.8 %copy-start.1 = (f32[1729,128]{1,0:T(8,128)S(1)}, f32[1729,128]{1,0:T(8,128)}, u32[]{:S(2)}) copy-start(f32[1729,128]{1,0:T(8,128)} %get-tuple-element.59) | copy-start | bytes 2655748
